TPU v7x, 256 devices: a whole 4x4x8 slice. The times are simulated.
256 devices in a mesh: ep: 32 (over z, x_lo, core), dp: 8 (over y, x_hi).
Axes of the slice: x: 4 (x_hi: 2, x_lo: 2; x = x_hi * 2 + x_lo), y: 4, z: 8, core: 2. Of those that a mesh axis runs over, the one named last changes fastest.
Arguments:
- grad_out: bfloat16 [49152, 3584], P(('ep', 'dp')), may hold values from -0.59765625 to 0.59765625
- route_probs: float32 [49152, 8], P(('ep', 'dp')), may hold values from 0.02 to 0.6
- routes: int32 [49152, 8], P(('ep', 'dp')), may hold values from 0 to 127, as said below
- hidden_saved: bfloat16 [256, 768, 2048], P(('ep', 'dp')), may hold values from -6 to 6
Outputs:
- grad_down: bfloat16 [2048, 114688], P('dp', 'ep')
Inputs may be any that keep to these rules, and one draw needn't show every extreme that they name: `routes`: each row names 8 different experts. In each aligned block of 192 rows (the rows of one device) no expert is named by more than 24 rows, and one expert whose index modulo 4 is below 1 is named by exactly 24 rows in every block.
All inputs are finite; a program needn't handle non-finite values.
Results may differ from a plain program's by a relative error of at most 0.015.
Values may be sent and summed in bfloat16 or wider, within the bound.
No kernel may reach another device: no remote copies, remote signals or barrier semaphores. Data moves between devices by JAX's collectives and lax.ppermute only.
A program may use at most 64 MiB of HBM per device.

v0:
```python
import jax
import jax.numpy as jnp
from jax import lax
from jax.sharding import PartitionSpec as P

EXP_DEV = 4


def expert_term(hidden_rows, arrived):
    return lax.dot_general(
        hidden_rows, arrived, (((0,), (0,)), ((), ())), preferred_element_type=jnp.float32
    )


def members_term(hidden_saved, arrived):
    parts = expert_term(hidden_saved[0], arrived[0])
    return parts


def shards(grad_out, route_probs, routes, hidden_saved):
    tok_rows, model_cols = grad_out.shape
    flight, slot_count, hidden = hidden_saved.shape
    expert_ranks = lax.axis_size("ep")
    capacity = slot_count // expert_ranks
    columns = expert_ranks * flight
    local_index = routes % EXP_DEV
    owner_rank = routes // EXP_DEV
    in_flight = local_index < flight
    column = jnp.where(in_flight, local_index * expert_ranks + owner_rank, columns)
    expert_ids = jnp.arange(columns + 1, dtype=jnp.int32)
    naming = jnp.sum((column[:, :, None] == expert_ids[None, None, :]).astype(jnp.int32), axis=1)
    earlier = jnp.cumsum(naming, axis=0) - naming
    position = jnp.take_along_axis(earlier, column, axis=1)
    target = jnp.where(in_flight, column * capacity + position, columns * capacity).reshape(-1)
    row_index = jnp.broadcast_to(
        jnp.arange(tok_rows, dtype=jnp.int32)[:, None], routes.shape
    ).reshape(-1)
    source_row = jnp.zeros((columns * capacity,), jnp.int32).at[target].set(row_index, mode="drop")
    weight = (
        jnp.zeros((columns * capacity,), jnp.float32)
        .at[target]
        .set(route_probs.reshape(-1), mode="drop")
    )
    scaled = (weight[:, None] * grad_out[source_row].astype(jnp.float32)).astype(jnp.bfloat16)
    outgoing = scaled.reshape(flight, expert_ranks, capacity, model_cols)
    arrived = lax.all_to_all(outgoing, "ep", split_axis=1, concat_axis=2, tiled=True).reshape(
        flight, slot_count, model_cols
    )
    summed = lax.psum_scatter(
        members_term(hidden_saved, arrived).astype(jnp.bfloat16),
        "dp",
        scatter_dimension=0,
        tiled=True,
    )
    return summed


def solution(mesh):
    in_specs = (
        P(("ep", "dp"), None),
        P(("ep", "dp"), None),
        P(("ep", "dp"), None),
        P(("ep", "dp"), None, None),
    )
    out_specs = P("dp", "ep")
    return jax.shard_map(shards, mesh=mesh, in_specs=in_specs, out_specs=out_specs, check_vma=False)
```

profile of v0, /device:TPU:32, one launch (start us, length us, event | category | flops | bytes accessed | tf_op | source)
XLA Modules:
  0.0 384.0 jit_solution(9815102031505101088)
XLA Ops:
  6.5 0.0 copy-start
  6.5 0.0 reduce-scatter.2.cloned.1.call-start
  6.5 0.9 copy.28
  7.5 0.8 copy.37
  8.3 0.7 reshape.113
  9.0 0.7 reshape.121
  9.7 0.1 bitcast_or_fusion
  9.9 0.1 reshape.103
  10.0 0.1 copy.32
  10.0 0.1 convert_reduce_fusion
  10.1 0.1 copy.36
  10.3 0.6 reduce-window.6
  10.9 0.2 slice_reduce_fusion
  11.1 0.1 broadcast_add_fusion
  11.2 0.8 copy.40
  12.0 0.9 slice_subtract_fusion
  12.9 10.3 %gather_fusion.1 = s32[1536]{0:T(1024)S(1)} fusion(s32[192,33]{1,0:T(8,128)S(1)} %slice_subtract_fusion, s32[1536]{0:T(1024)S(1)} %reshape.103), kind=kCustom, calls=%fused_computation.1 | custom fusion | bytes 24576 | tf_op jit(solution)/shard_map/jit(take_along_axis)/gather | solution.py:33
  23.2 0.1 reshape.106
  23.3 0.1 add_select_fusion.2
  23.4 0.1 reshape.91
  23.6 6.3 %scatter_custom_fusion.1 = s32[768]{0:T(1024)S(1)} fusion(s32[1536]{0:T(1024)S(1)} %fusion.8, s32[1536]{0:T(1024)} %reshape.121, s32[]{:T(128)} %constant.49.clone.1), kind=kCustom, calls=%fused_computation.32 | custom fusion | bytes 3584 | tf_op jit(solution)/shard_map/scatter | solution.py:38
  29.9 6.3 %scatter_custom_fusion = f32[768]{0:T(1024)S(1)} fusion(s32[1536]{0:T(1024)S(1)} %fusion.8, f32[1536]{0:T(1024)} %reshape.113, f32[]{:T(128)} %constant.48.clone.1), kind=kCustom, calls=%fused_computation.34 | custom fusion | bytes 3584 | tf_op jit(solution)/shard_map/scatter | solution.py:42
  36.3 0.1 mul.33
  36.4 12.5 %gather_fusion = bf16[768,3584]{1,0:T(8,128)(2,1)} fusion(bf16[192,3584]{1,0:T(8,128)(2,1)} %param.4, s32[1024]{0:T(1024)S(1)} %pad_clamp_fusion), kind=kCustom, calls=%fused_computation | custom fusion | bytes 11013120 | tf_op jit(solution)/shard_map/gather | solution.py:44
  48.9 4.3 %fusion.1 = bf16[1,32,24,3584]{3,2,0,1:T(8,128)(2,1)S(1)} fusion(bf16[1,32,24,3584]{3,2,0,1:T(8,128)(2,1)} %bitcast.22, f32[32,24]{1,0:T(8,128)S(1)} %mul.33), kind=kLoop, calls=%fused_computation.7 | loop fusion | flops 8257536 | bytes 11013120 | tf_op jit(solution)/shard_map/convert_element_type | solution.py:44
  53.2 133.1 %all_to_all.4 = bf16[1,32,24,3584]{3,2,0,1:T(8,128)(2,1)S(1)} all-to-all(bf16[1,32,24,3584]{3,2,0,1:T(8,128)(2,1)S(1)} %fusion.1), channel_id=1, replica_groups=mesh['ep'=32,'dp'=8] {'ep'}, dimensions={1} | all-to-all | bytes 11010048 | tf_op jit(solution)/shard_map/all_to_all | solution.py:46
  186.3 0.0 copy-done
  186.3 14.3 %fusion = bf16[2048,3584]{0,1:T(8,128)(2,1)} fusion(bf16[768,3584]{1,0:T(8,128)(2,1)S(1)} %bitcast.23, bf16[1,768,2048]{2,1,0:T(8,128)(2,1)S(1)} %copy-done), kind=kOutput, calls=%fused_computation.5 | convolution fusion | flops 11281629184 | bytes 23330816 | tf_op jit(solution)/shard_map/dot_general | solution.py:10
  200.6 0.0 reduce-scatter.2.cloned.1.call-update
  200.6 172.7 %reduce-scatter.2.cloned.1.call-done = bf16[256,3584]{0,1:T(8,128)(2,1)} async-done(((bf16[2048,3584]{0,1:T(8,128)(2,1)}), bf16[256,3584]{0,1:T(8,128)(2,1)}) %reduce-scatter.2.cloned.1.call-update) | async-done | bytes 1835024 | tf_op jit(solution)/shard_map/reduce_scatter | solution.py:49
  373.3 3.8 copy.39
  (9 shorter events, 0.1 us)
Async XLA Ops:
  6.5 179.8 %copy-start = (bf16[1,768,2048]{2,1,0:T(8,128)(2,1)S(1)}, bf16[1,768,2048]{2,1,0:T(8,128)(2,1)}, u32[]{:S(2)}) copy-start(bf16[1,768,2048]{2,1,0:T(8,128)(2,1)} %param.7) | copy-start | bytes 9437188
  6.5 366.8 %reduce-scatter.2.cloned.1.call-start = ((), (), s32[]{:S(2)}) async-start(), calls=%async_computation.2 | async-start | bytes 16515072 | tf_op jit(solution)/shard_map/reduce_scatter | solution.py:49
Sparse Core Ops, SparseCore 0:
  200.7 172.5 reduce-scatter.1
where the time goes:
time: 385 us; the launch traced here: 384 us
  waiting for transfers between devices  173 us (45%)
  blocking collectives  133 us (35%)
  local copies, waits for them, and re-layouts  44 us (11%)
  matrix products  14.3 us (4%)
  between operations  13.5 us (4%)
  other arithmetic  6.3 us (2%)
    reduce_scatter x1, waiting for transfers between devices, shards(): lax.psum_scatter(members_term(hidden_saved, arrived).astype(jnp.bfloat16)...  173 us
    all_to_all x1, blocking collectives, shards(): lax.all_to_all(outgoing, 'ep', split_axis=1, concat_axis=2, tiled=True)  133 us
    dot_general x1, matrix products, expert_term(): lax.dot_general(hidden_rows, arrived, (((0,), (0,)), ((), ())), preferred...  14.3 us
    gather x1, local copies, waits for them, and re-layouts, shards(): grad_out[source_row].astype(jnp.float32)  12.5 us
    gather x3, local copies, waits for them, and re-layouts, shards(): position = jnp.take_along_axis(earlier, column, axis=1)  10.5 us
  transfers between devices with their start and end apart: 1, of which 1 were waited for; matrix products, arithmetic and copies ran while one was open for 0% of the time, Pallas kernels for 0%

commit v1 on v0

v1 whole, which is shorter than its diff:
```python
import functools

import jax
import jax.numpy as jnp
from jax import lax
from jax.experimental import pallas as pl
from jax.experimental.pallas import tpu as pltpu
from jax.sharding import PartitionSpec as P

EXP_DEV = 4
CHUNKS = 4


def rows_kernel(columns, capacity, chunks, routes_ref, probs_ref, grad_ref, *out_refs):
    top, tok = routes_ref.shape
    ids = lax.broadcasted_iota(jnp.int32, (columns, tok), 0) * EXP_DEV
    named = jnp.zeros((columns, tok), jnp.float32)
    prob = jnp.zeros((columns, tok), jnp.float32)
    for k in range(top):
        hit = routes_ref[k : k + 1, :] == ids
        named = named + jnp.where(hit, 1.0, 0.0)
        prob = prob + jnp.where(hit, probs_ref[k : k + 1, :], 0.0)
    row = lax.broadcasted_iota(jnp.int32, (tok, tok), 0)
    col = lax.broadcasted_iota(jnp.int32, (tok, tok), 1)
    earlier = jnp.where(row < col, 1.0, 0.0).astype(jnp.bfloat16)
    slot = jnp.dot(named.astype(jnp.bfloat16), earlier, preferred_element_type=jnp.float32)
    slot = jnp.where(named > 0.0, slot, -1.0).astype(jnp.int32)
    places = lax.broadcasted_iota(jnp.int32, (columns, capacity, tok), 1)
    pick = slot[:, None, :] == places
    weight = jnp.sum(jnp.where(pick, prob[:, None, :], 0.0), axis=2, keepdims=True)
    weight = weight.reshape(columns * capacity, 1)
    pick = jnp.where(pick, 1.0, 0.0).reshape(columns * capacity, tok).astype(jnp.bfloat16)
    width = grad_ref.shape[1] // chunks
    for c in range(chunks):
        taken = jnp.dot(
            pick, grad_ref[:, c * width : (c + 1) * width], preferred_element_type=jnp.float32
        )
        out_refs[c][...] = (weight * taken).astype(jnp.bfloat16)


def expert_term(hidden_rows, arrived):
    return lax.dot_general(
        hidden_rows, arrived, (((0,), (0,)), ((), ())), preferred_element_type=jnp.float32
    ).astype(jnp.bfloat16)


def shards(grad_out, route_probs, routes, hidden_saved):
    tok, model_cols = grad_out.shape
    flight, slot_count, hidden = hidden_saved.shape
    ranks = lax.axis_size("ep")
    capacity = slot_count // ranks
    width = model_cols // CHUNKS
    outgoing = pl.pallas_call(
        functools.partial(rows_kernel, ranks, capacity, CHUNKS),
        out_shape=[jax.ShapeDtypeStruct((slot_count, width), jnp.bfloat16)] * CHUNKS,
        compiler_params=pltpu.CompilerParams(vmem_limit_bytes=48 * 1024 * 1024),
    )(routes.T, route_probs.T, grad_out)
    parts = []
    for c in range(CHUNKS):
        rows = outgoing[c].reshape(ranks, capacity, width)
        arrived = lax.all_to_all(rows, "ep", split_axis=0, concat_axis=0, tiled=True)
        term = expert_term(hidden_saved[0], arrived.reshape(slot_count, width))
        parts.append(lax.psum_scatter(term, "dp", scatter_dimension=0, tiled=True))
    return jnp.concatenate(parts, axis=1)


def solution(mesh):
    in_specs = (
        P(("ep", "dp"), None),
        P(("ep", "dp"), None),
        P(("ep", "dp"), None),
        P(("ep", "dp"), None, None),
    )
    return jax.shard_map(
        shards, mesh=mesh, in_specs=in_specs, out_specs=P("dp", "ep"), check_vma=False
    )
```

time: 385 us -> 449 us (1.17)
  waiting for transfers between devices: 173 us -> 237 us
  local copies, waits for them, and re-layouts: 44 us -> 8.77 us
  blocking collectives: 133 us -> 165 us
    reduce_scatter x1 -> x4, waiting for transfers between devices: 173 us -> 237 us  [shards(): parts.append(lax.psum_scatter(term, 'dp', scatter_dimension=0, tiled=True))]
    all_to_all x1 -> x4, blocking collectives: 133 us -> 165 us  [shards(): lax.all_to_all(rows, 'ep', split_axis=0, concat_axis=0, tiled=True)]
    gather x4 -> x0, local copies, waits for them, and re-layouts: 23 us -> none  [the longest x1 12.5 us: shards(): grad_out[source_row].astype(jnp.float32)]
    scatter x2 -> x0, local copies, waits for them, and re-layouts: 12.7 us -> none  [the longest x1 6.34 us: shards(): jnp.zeros((columns * capacity,), jnp.int32).at[target]]
    dot_general x1 -> x4, matrix products: 14.3 us -> 18.2 us  [expert_term(): lax.dot_general(hidden_rows, arrived, (((0,), (0,)), ((), ())), preferred...]
  transfers between devices with their start and end apart: 1 -> 4, of which waited for: 1 -> 3; matrix products, arithmetic and copies ran while one was open for 0% -> 3% of each run, Pallas kernels for 0% -> 0%
where the time goes in v1:
time: 449 us
  waiting for transfers between devices  237 us (53%)
  blocking collectives  165 us (37%)
  matrix products  18.2 us (4%)
  between operations  13.2 us (3%)
  local copies, waits for them, and re-layouts  8.77 us (2%)
    reduce_scatter x4, waiting for transfers between devices, shards(): parts.append(lax.psum_scatter(term, 'dp', scatter_dimension=0, tiled=True))  237 us
    all_to_all x4, blocking collectives, shards(): lax.all_to_all(rows, 'ep', split_axis=0, concat_axis=0, tiled=True)  165 us
    dot_general x4, matrix products, expert_term(): lax.dot_general(hidden_rows, arrived, (((0,), (0,)), ((), ())), preferred...  18.2 us
  transfers between devices with their start and end apart: 4, of which 3 were waited for; matrix products, arithmetic and copies ran while one was open for 3% of the time, Pallas kernels for 0%

profile of v1, /device:TPU:32, one launch (start us, length us, event | category | flops | bytes accessed | tf_op | source)
XLA Modules:
  0.0 448.8 jit_solution(6208712616239821978)
XLA Ops:
  6.5 0.0 copy-start
  6.5 0.0 reduce-scatter.11.cloned.1.call-start
  6.5 0.0 copy-start.4
  6.5 0.8 copy-done.4
  7.4 0.0 copy-start.5
  7.4 0.8 copy-done.5
  8.2 3.3 shard_map.46
  11.5 0.0 copy-start.1
  11.5 1.1 copy-done.1
  12.6 0.0 copy-start.2
  12.6 1.2 copy-done.2
  13.8 0.0 copy-start.3
  13.8 1.1 copy-done.3
  14.8 44.5 %all_to_all.20 = bf16[32,24,896]{2,1,0:T(8,128)(2,1)S(1)} all-to-all(bf16[32,24,896]{2,1,0:T(8,128)(2,1)S(1)} %bitcast.34), channel_id=1, replica_groups=mesh['ep'=32,'dp'=8] {'ep'}, dimensions={0} | all-to-all | bytes 2752512 | tf_op jit(solution)/shard_map/all_to_all | solution.py:61
  59.4 0.0 copy-done
  59.4 4.5 %convert_bitcast_fusion = bf16[2048,896]{0,1:T(8,128)(2,1)} fusion(bf16[768,896]{1,0:T(8,128)(2,1)S(1)} %bitcast.37, bf16[1,768,2048]{2,1,0:T(8,128)(2,1)S(1)} %copy-done), kind=kOutput, calls=%fused_computation | convolution fusion | flops 2820407296 | bytes 8192000 | tf_op jit(solution)/shard_map/dot_general | solution.py:42
  63.9 0.0 reduce-scatter.11.cloned.1.call-update
  63.9 0.0 reduce-scatter.9.cloned.1.call-start
  64.0 40.1 %all_to_all.21 = bf16[32,24,896]{2,1,0:T(8,128)(2,1)S(1)} all-to-all(bf16[32,24,896]{2,1,0:T(8,128)(2,1)} %bitcast.33), channel_id=1, replica_groups=mesh['ep'=32,'dp'=8] {'ep'}, dimensions={0} | all-to-all | bytes 2752512 | tf_op jit(solution)/shard_map/all_to_all | solution.py:61
  104.1 4.5 %convert_bitcast_fusion.1 = bf16[2048,896]{0,1:T(8,128)(2,1)} fusion(bf16[768,896]{1,0:T(8,128)(2,1)S(1)} %bitcast.38, bf16[1,768,2048]{2,1,0:T(8,128)(2,1)S(1)} %copy-done), kind=kOutput, calls=%fused_computation.1 | convolution fusion | flops 2820407296 | bytes 8192000 | tf_op jit(solution)/shard_map/dot_general | solution.py:42
  108.6 0.0 reduce-scatter.9.cloned.1.call-update
  108.6 0.0 reduce-scatter.5.cloned.1.call-start
  108.7 40.2 %all_to_all.22 = bf16[32,24,896]{2,1,0:T(8,128)(2,1)S(1)} all-to-all(bf16[32,24,896]{2,1,0:T(8,128)(2,1)} %bitcast.32), channel_id=1, replica_groups=mesh['ep'=32,'dp'=8] {'ep'}, dimensions={0} | all-to-all | bytes 2752512 | tf_op jit(solution)/shard_map/all_to_all | solution.py:61
  148.9 4.6 %convert_bitcast_fusion.3 = bf16[2048,896]{0,1:T(8,128)(2,1)} fusion(bf16[768,896]{1,0:T(8,128)(2,1)S(1)} %bitcast.39, bf16[1,768,2048]{2,1,0:T(8,128)(2,1)S(1)} %copy-done), kind=kOutput, calls=%fused_computation.3 | convolution fusion | flops 2820407296 | bytes 8192000 | tf_op jit(solution)/shard_map/dot_general | solution.py:42
  153.5 0.0 reduce-scatter.5.cloned.1.call-update
  153.5 0.0 reduce-scatter.7.cloned.1.call-start
  153.6 40.2 %all_to_all.23 = bf16[32,24,896]{2,1,0:T(8,128)(2,1)S(1)} all-to-all(bf16[32,24,896]{2,1,0:T(8,128)(2,1)} %bitcast.31), channel_id=1, replica_groups=mesh['ep'=32,'dp'=8] {'ep'}, dimensions={0} | all-to-all | bytes 2752512 | tf_op jit(solution)/shard_map/all_to_all | solution.py:61
  193.8 4.5 %convert_bitcast_fusion.2 = bf16[2048,896]{0,1:T(8,128)(2,1)} fusion(bf16[768,896]{1,0:T(8,128)(2,1)S(1)} %bitcast.40, bf16[1,768,2048]{2,1,0:T(8,128)(2,1)S(1)} %copy-done), kind=kOutput, calls=%fused_computation.2 | convolution fusion | flops 2820407296 | bytes 8192000 | tf_op jit(solution)/shard_map/dot_general | solution.py:42
  198.3 0.0 reduce-scatter.7.cloned.1.call-update
  198.3 0.0 reduce-scatter.11.cloned.1.call-done
  198.3 56.9 %reduce-scatter.9.cloned.1.call-done = bf16[256,896]{0,1:T(8,128)(2,1)} async-done(((bf16[2048,896]{0,1:T(8,128)(2,1)}), bf16[256,896]{0,1:T(8,128)(2,1)}) %reduce-scatter.9.cloned.1.call-update) | async-done | bytes 458768 | tf_op jit(solution)/shard_map/reduce_scatter | solution.py:63
  255.2 90.3 %reduce-scatter.5.cloned.1.call-done = bf16[256,896]{0,1:T(8,128)(2,1)} async-done(((bf16[2048,896]{0,1:T(8,128)(2,1)}), bf16[256,896]{0,1:T(8,128)(2,1)}) %reduce-scatter.5.cloned.1.call-update) | async-done | bytes 458768 | tf_op jit(solution)/shard_map/reduce_scatter | solution.py:63
  345.5 90.2 %reduce-scatter.7.cloned.1.call-done = bf16[256,896]{0,1:T(8,128)(2,1)} async-done(((bf16[2048,896]{0,1:T(8,128)(2,1)}), bf16[256,896]{0,1:T(8,128)(2,1)}) %reduce-scatter.7.cloned.1.call-update) | async-done | bytes 458768 | tf_op jit(solution)/shard_map/reduce_scatter | solution.py:63
  435.7 2.8 pad_maximum_fusion
  438.5 3.8 copy.5
Async XLA Ops:
  6.5 52.8 %copy-start = (bf16[1,768,2048]{2,1,0:T(8,128)(2,1)S(1)}, bf16[1,768,2048]{2,1,0:T(8,128)(2,1)}, u32[]{:S(2)}) copy-start(bf16[1,768,2048]{2,1,0:T(8,128)(2,1)} %param.7) | copy-start | bytes 9437188
  6.5 191.8 %reduce-scatter.11.cloned.1.call-start = ((), (), s32[]{:S(2)}) async-start(), calls=%async_computation.11 | async-start | bytes 4128768 | tf_op jit(solution)/shard_map/reduce_scatter | solution.py:63
  6.5 0.8 copy-start.4
  7.4 0.8 copy-start.5
  11.5 1.1 copy-start.1
  12.6 1.2 copy-start.2
  13.8 1.1 copy-start.3
  63.9 191.3 %reduce-scatter.9.cloned.1.call-start = ((), (), s32[]{:S(2)}) async-start(), calls=%async_computation.10 | async-start | bytes 4128768 | tf_op jit(solution)/shard_map/reduce_scatter | solution.py:63
  108.6 236.9 %reduce-scatter.5.cloned.1.call-start = ((), (), s32[]{:S(2)}) async-start(), calls=%async_computation.8 | async-start | bytes 4128768 | tf_op jit(solution)/shard_map/reduce_scatter | solution.py:63
  153.5 282.1 %reduce-scatter.7.cloned.1.call-start = ((), (), s32[]{:S(2)}) async-start(), calls=%async_computation.9 | async-start | bytes 4128768 | tf_op jit(solution)/shard_map/reduce_scatter | solution.py:63
Sparse Core Ops, SparseCore 0:
  64.0 98.2 reduce-scatter.10
  166.6 88.5 reduce-scatter.8
  259.4 86.0 reduce-scatter.4
  349.6 86.0 reduce-scatter.6

commit v2 on v1

v2 whole, which is shorter than its diff:
```python
import functools

import jax
import jax.numpy as jnp
from jax import lax
from jax.experimental import pallas as pl
from jax.experimental.pallas import tpu as pltpu
from jax.sharding import PartitionSpec as P

EXP_DEV = 4
WIDTHS = (768, 1280, 1024, 512)
VMEM = 56 * 1024 * 1024
SPARE = 10 * 1024 * 1024


def rows_kernel(columns, capacity, widths, routes_ref, probs_ref, grad_ref, *out_refs):
    top, tok = routes_ref.shape
    ids = lax.broadcasted_iota(jnp.int32, (columns, tok), 0) * EXP_DEV
    named = jnp.zeros((columns, tok), jnp.float32)
    prob = jnp.zeros((columns, tok), jnp.float32)
    for k in range(top):
        hit = routes_ref[k : k + 1, :] == ids
        named = named + jnp.where(hit, 1.0, 0.0)
        prob = prob + jnp.where(hit, probs_ref[k : k + 1, :], 0.0)
    row = lax.broadcasted_iota(jnp.int32, (tok, tok), 0)
    col = lax.broadcasted_iota(jnp.int32, (tok, tok), 1)
    earlier = jnp.where(row < col, 1.0, 0.0).astype(jnp.bfloat16)
    slot = jnp.dot(named.astype(jnp.bfloat16), earlier, preferred_element_type=jnp.float32)
    slot = jnp.where(named > 0.0, slot, -1.0).astype(jnp.int32)
    places = lax.broadcasted_iota(jnp.int32, (columns, capacity, tok), 1)
    pick = slot[:, None, :] == places
    weight = jnp.sum(jnp.where(pick, prob[:, None, :], 0.0), axis=2, keepdims=True)
    weight = weight.reshape(columns * capacity, 1)
    pick = jnp.where(pick, 1.0, 0.0).reshape(columns * capacity, tok).astype(jnp.bfloat16)
    start = 0
    for c, width in enumerate(widths):
        taken = jnp.dot(
            pick, grad_ref[:, start : start + width], preferred_element_type=jnp.float32
        )
        out_refs[c][...] = (weight * taken).astype(jnp.bfloat16)
        start += width


def product(hidden_ref, at, size, rows):
    return lax.dot_general(
        hidden_ref[:, pl.ds(pl.multiple_of(at, size), size)],
        rows,
        (((0,), (0,)), ((), ())),
        preferred_element_type=jnp.float32,
    )


def first_terms(place, hidden_ref, ins, outs):
    (arrived_ref,) = ins
    size = hidden_ref.shape[1] // 4
    half = arrived_ref.shape[1] // 2
    y = place[0]
    one, two = y ^ 1, 3 - y
    for h, near in enumerate((one, two)):
        rows = arrived_ref[:, h * half : (h + 1) * half]
        for i, block in enumerate((two ^ 1, near)):
            outs[h][i * size : (i + 1) * size, :] = product(
                hidden_ref, block * size, size, rows
            ).astype(jnp.bfloat16)


def second_terms(place, hidden_ref, ins, outs):
    arrived_ref, *got = ins
    size = hidden_ref.shape[1] // 4
    half = arrived_ref.shape[1] // 2
    y = place[0]
    for h, far in enumerate((3 - y, y ^ 1)):
        rows = arrived_ref[:, h * half : (h + 1) * half]
        mine = product(hidden_ref, far * size, size, rows)
        outs[h][...] = (mine + got[h][:size, :].astype(jnp.float32)).astype(jnp.bfloat16)


def third_terms(place, hidden_ref, ins, outs):
    arrived_ref, *rest = ins
    got, more = rest[:2], rest[2:]
    size = hidden_ref.shape[1] // 4
    part = size // 2
    half = arrived_ref.shape[1] // 2
    y, xh = place[0], place[1]
    for out_ref, x in zip(outs, (1 - xh, xh)):
        at = pl.multiple_of(x * part, part)
        for h in range(2):
            cols = slice(h * half, (h + 1) * half)
            total = product(hidden_ref, y * size + x * part, part, arrived_ref[:, cols])
            total = total + got[h][pl.ds(size + at, part), :].astype(jnp.float32)
            total = total + more[h][pl.ds(at, part), :].astype(jnp.float32)
            out_ref[:, cols] = total.astype(out_ref.dtype)


def last_sum(place, hidden_ref, ins, outs):
    keep_ref, last_ref = ins
    outs[0][...] = (keep_ref[...] + last_ref[...].astype(jnp.float32)).astype(jnp.bfloat16)


def tick_kernel(jobs, passed, place_ref, hidden_ref, *refs):
    ins = refs[: sum(n for _, n, _ in jobs)]
    outs = refs[len(ins) + passed :]
    i = o = 0
    for job, n_in, n_out in jobs:
        job(place_ref, hidden_ref, ins[i : i + n_in], outs[o : o + n_out])
        i, o = i + n_in, o + n_out


def tick(place, hidden, jobs, passed):
    ins = [x for _, given, _ in jobs for x in given]
    shapes = [s for _, _, made in jobs for s in made]
    counts = [(job, len(given), len(made)) for job, given, made in jobs]
    vmem, anywhere = pl.BlockSpec(memory_space=pltpu.VMEM), pl.BlockSpec(memory_space=pl.ANY)
    held = sum(x.size * x.dtype.itemsize for x in [hidden, *ins, *shapes])
    res = pl.pallas_call(
        functools.partial(tick_kernel, counts, len(passed)),
        in_specs=[pl.BlockSpec(memory_space=pltpu.SMEM), vmem]
        + [vmem] * len(ins)
        + [anywhere] * len(passed),
        out_specs=[vmem] * len(shapes) + [anywhere] * len(passed),
        out_shape=shapes + [jax.ShapeDtypeStruct(p.shape, p.dtype) for p in passed],
        input_output_aliases={2 + len(ins) + i: len(shapes) + i for i in range(len(passed))},
        compiler_params=pltpu.CompilerParams(vmem_limit_bytes=min(VMEM, held + SPARE)),
    )(place, hidden, *ins, *passed)
    made, at = [], 0
    for _, _, n_out in counts:
        made.append(res[at : at + n_out])
        at += n_out
    return made, res[at:]


def shards(grad_out, route_probs, routes, hidden_saved):
    tok, model_cols = grad_out.shape
    flight, slot_count, hidden = hidden_saved.shape
    ranks = lax.axis_size("ep")
    peers = lax.axis_size("dp")
    capacity = slot_count // ranks
    dp = lax.axis_index("dp")
    place = jnp.stack([dp // 2, dp % 2]).astype(jnp.int32)
    outgoing = pl.pallas_call(
        functools.partial(rows_kernel, ranks, capacity, WIDTHS),
        out_shape=[jax.ShapeDtypeStruct((slot_count, w), jnp.bfloat16) for w in WIDTHS],
        compiler_params=pltpu.CompilerParams(vmem_limit_bytes=VMEM),
    )(routes.T, route_probs.T, grad_out)

    to_a = [(i, i ^ 2) for i in range(peers)]
    to_b = [(i, (3 - i // 2) * 2 + i % 2) for i in range(peers)]
    to_x = [(i, i ^ 1) for i in range(peers)]
    hid = hidden_saved[0]
    count = len(WIDTHS)

    def shape(rows, cols, dtype=jnp.bfloat16):
        return jax.ShapeDtypeStruct((rows, cols), dtype)

    arrived, got, more, keep, last, out = {}, {}, {}, {}, {}, {}
    rows = outgoing[0]
    for t in range(count + 4):
        if t > 0:
            jobs, chunks = [], []
            for back, body in ((1, first_terms), (2, second_terms), (3, third_terms), (4, last_sum)):
                c = t - back
                if not 0 <= c < count:
                    continue
                w = WIDTHS[c]
                if back == 1:
                    job = (body, [arrived[c]], [shape(hidden // 2, w // 2)] * 2)
                elif back == 2:
                    job = (body, [arrived[c], *got[c]], [shape(hidden // 4, w // 2)] * 2)
                elif back == 3:
                    job = (
                        body,
                        [arrived[c], *got[c], *more[c]],
                        [shape(hidden // peers, w), shape(hidden // peers, w, jnp.float32)],
                    )
                else:
                    job = (body, [keep[c], last[c]], [shape(hidden // peers, w)])
                jobs.append(job)
                chunks.append((back, c))
            passed = [outgoing[t]] if t < count else []
            made, passed = tick(place, hid, jobs, passed)
            for (back, c), made_here in zip(chunks, made):
                if back == 1:
                    got[c] = [lax.ppermute(s, "dp", to) for s, to in zip(made_here, (to_a, to_b))]
                elif back == 2:
                    more[c] = [lax.ppermute(s, "dp", to) for s, to in zip(made_here, (to_b, to_a))]
                elif back == 3:
                    last[c], keep[c] = lax.ppermute(made_here[0], "dp", to_x), made_here[1]
                else:
                    out[c] = made_here[0]
            if t < count:
                rows = passed[0]
        if t < count:
            came = lax.all_to_all(
                rows.reshape(ranks, capacity, WIDTHS[t]), "ep", split_axis=0, concat_axis=0, tiled=True
            )
            arrived[t] = came.reshape(slot_count, WIDTHS[t])
    return jnp.concatenate([out[c] for c in range(count)], axis=1)


def solution(mesh):
    in_specs = (
        P(("ep", "dp"), None),
        P(("ep", "dp"), None),
        P(("ep", "dp"), None),
        P(("ep", "dp"), None, None),
    )
    return jax.shard_map(
        shards, mesh=mesh, in_specs=in_specs, out_specs=P("dp", "ep"), check_vma=False
    )
```

time: 449 us -> 316 us (0.70)
  blocking collectives: 165 us -> 0 us
  starting transfers between devices: 0.13 us -> 55.9 us
  waiting for transfers between devices: 237 us -> 183 us
  local copies, waits for them, and re-layouts: 8.77 us -> 43.2 us
  Pallas kernels: 3.31 us -> 31.3 us
  matrix products: 18.2 us -> 0 us
  between operations: 13.2 us -> 0.2 us
    reduce_scatter x4 -> x0, waiting for transfers between devices: 237 us -> none  [shards(): parts.append(lax.psum_scatter(term, 'dp', scatter_dimension=0, tiled=True))]
    all_to_all x4 -> x0, blocking collectives: 165 us -> none  [shards(): lax.all_to_all(rows, 'ep', split_axis=0, concat_axis=0, tiled=True)]
    ppermute x0 -> x20, waiting for transfers between devices: none -> 127 us  [the longest x16 101 us: shards(): lax.ppermute(s, 'dp', to)]
    all_to_all x0 -> x4, waiting for transfers between devices: none -> 55.4 us  [shards(): lax.all_to_all(rows.reshape(ranks, capacity, WIDTHS[t]), 'ep', split_axis...]
    unnamed x12 -> x84, local copies, waits for them, and re-layouts: 4.98 us -> 43.2 us
    all_to_all x0 -> x4, starting transfers between devices: none -> 29.5 us  [shards(): lax.all_to_all(rows.reshape(ranks, capacity, WIDTHS[t]), 'ep', split_axis...]
    pallas_call x1 -> x8, Pallas kernels: 3.31 us -> 31.3 us  [the longest x7 26.5 us: tick(): pl.pallas_call(functools.partial(tick_kernel, counts, len(passed)), in_sp...]
    ppermute x0 -> x20, starting transfers between devices: none -> 26.5 us  [the longest x16 19.2 us: shards(): lax.ppermute(s, 'dp', to)]
  transfers between devices with their start and end apart: 4 -> 24, of which waited for: 3 -> 14; matrix products, arithmetic and copies ran while one was open for 3% -> 0% of each run, Pallas kernels for 0% -> 0%
where the time goes in v2:
time: 316 us; the launch traced here: 315 us
  waiting for transfers between devices  183 us (58%)
  starting transfers between devices  55.9 us (18%)
  local copies, waits for them, and re-layouts  43.2 us (14%)
  Pallas kernels  31.3 us (10%)
    ppermute x16, waiting for transfers between devices, shards(): lax.ppermute(s, 'dp', to)  101 us
    all_to_all x4, waiting for transfers between devices, shards(): lax.all_to_all(rows.reshape(ranks, capacity, WIDTHS[t]), 'ep', split_axis...  55.4 us
    unnamed x84, local copies, waits for them, and re-layouts  43.2 us
    all_to_all x4, starting transfers between devices, shards(): lax.all_to_all(rows.reshape(ranks, capacity, WIDTHS[t]), 'ep', split_axis...  29.5 us
    pallas_call x7, Pallas kernels, tick(): pl.pallas_call(functools.partial(tick_kernel, counts, len(passed)), in_sp...  26.5 us
    ppermute x4, waiting for transfers between devices, shards(): last[c], keep[c] = (lax.ppermute(made_here[0], 'dp', to_x), made_here[1])  25.8 us
    ppermute x16, starting transfers between devices, shards(): lax.ppermute(s, 'dp', to)  19.2 us
    ppermute x4, starting transfers between devices, shards(): last[c], keep[c] = (lax.ppermute(made_here[0], 'dp', to_x), made_here[1])  7.31 us
  transfers between devices with their start and end apart: 24, of which 14 were waited for; matrix products, arithmetic and copies ran while one was open for 0% of the time, Pallas kernels for 0%

profile of v2, /device:TPU:32, one launch (start us, length us, event | category | flops | bytes accessed | tf_op | source)
XLA Modules:
  0.0 314.6 jit_solution(14130561325430470554)
XLA Ops:
  0.0 4.8 %shard_map.46 = (bf16[768,768]{1,0:T(8,128)(2,1)}, bf16[768,1280]{1,0:T(8,128)(2,1)}, bf16[768,1024]{1,0:T(8,128)(2,1)}, bf16[768,512]{1,0:T(8,128)(2,1)}) custom-call(s32[8,192]{1,0:T(8,128)} %bitcast.24, f32[8,192]{1,0:T(8,128)} %bitcast.25, bf16[192,3584]{1,0:T(8,128)(2,1)} %grad_ref.1), custom_call_target="tpu_custom_call" | custom-call | tf_op jit(solution)/shard_map/pallas_call | solution.py:140
  4.8 9.7 %all-to-all-start = ((bf16[32,24,768]{2,1,0:T(8,128)(2,1)}), bf16[32,24,768]{2,1,0:T(8,128)(2,1)}, u32[]{:S(2)}, u32[]{:S(2)}) async-start(bf16[32,24,768]{2,1,0:T(8,128)(2,1)} %bitcast.23), calls=%async_computation | async-start | bytes 2359296 | tf_op jit(solution)/shard_map/all_to_all | solution.py:193
  14.6 30.8 %all-to-all-done = bf16[32,24,768]{2,1,0:T(8,128)(2,1)} async-done(((bf16[32,24,768]{2,1,0:T(8,128)(2,1)}), bf16[32,24,768]{2,1,0:T(8,128)(2,1)}, u32[]{:S(2)}, u32[]{:S(2)}) %all-to-all-start) | async-done | bytes 1179680 | tf_op jit(solution)/shard_map/all_to_all | solution.py:193
  45.4 1.5 copy-done.1
  47.0 3.1 shard_map.47
  50.1 1.3 copy-done.2
  53.2 5.6 %all-to-all-start.1 = ((bf16[32,24,1280]{2,1,0:T(8,128)(2,1)}), bf16[32,24,1280]{2,1,0:T(8,128)(2,1)}, u32[]{:S(2)}, u32[]{:S(2)}) async-start(bf16[32,24,1280]{2,1,0:T(8,128)(2,1)} %bitcast.20), calls=%async_computation.1 | async-start | bytes 3932160 | tf_op jit(solution)/shard_map/all_to_all | solution.py:193
  58.9 1.7 collective-permute-start
  60.5 2.2 collective-permute-start.1
  62.7 16.0 %collective-permute-done.refs_2_.refs_5_ = bf16[1024,384]{1,0:T(8,128)(2,1)S(1)} collective-permute-done((bf16[1024,384]{1,0:T(8,128)(2,1)}, bf16[1024,384]{1,0:T(8,128)(2,1)S(1)}, u32[]{:S(2)}, u32[]{:S(2)}) %collective-permute-start) | collective-permute-done | bytes 786464 | tf_op jit(solution)/shard_map/ppermute | solution.py:183
  79.6 1.6 collective-permute-done.1.refs_3_.refs_6_
  82.2 24.6 %all-to-all-done.1 = bf16[32,24,1280]{2,1,0:T(8,128)(2,1)} async-done(((bf16[32,24,1280]{2,1,0:T(8,128)(2,1)}), bf16[32,24,1280]{2,1,0:T(8,128)(2,1)}, u32[]{:S(2)}, u32[]{:S(2)}) %all-to-all-start.1) | async-done | bytes 1966112 | tf_op jit(solution)/shard_map/all_to_all | solution.py:193
  106.7 1.4 copy-done.3
  108.1 1.1 copy-done.16
  109.3 1.1 copy-done.19
  110.4 5.4 %shard_map.48 = (bf16[1024,640]{1,0:T(8,128)(2,1)S(1)}, bf16[1024,640]{1,0:T(8,128)(2,1)S(1)}, bf16[512,384]{1,0:T(8,128)(2,1)S(1)}, bf16[512,384]{1,0:T(8,128)(2,1)S(1)}, bf16[768,1024]{1,0:T(8,128)(2,1)S(1)}) custom-call(s32[2]{0:T(128)S(1)} %pad_add_fusion.place_ref, bf16[768,2048]{1,0:T(8,128)(2,1)S(1)} %bitcast.14, ...), custom_call_target="tpu_custom_call", output_to_operand_aliasing={{4}: (6, {})} | custom-call | tf_op jit(solution)/shard_map/pallas_call | solution.py:115
  115.8 1.1 copy-done.4
  120.6 5.7 %all-to-all-start.2 = ((bf16[32,24,1024]{2,1,0:T(8,128)(2,1)}), bf16[32,24,1024]{2,1,0:T(8,128)(2,1)}, u32[]{:S(2)}, u32[]{:S(2)}) async-start(bf16[32,24,1024]{2,1,0:T(8,128)(2,1)} %bitcast.21), calls=%async_computation.2 | async-start | bytes 3145728 | tf_op jit(solution)/shard_map/all_to_all | solution.py:193
  126.4 1.7 collective-permute-start.2
  128.0 2.2 collective-permute-start.3
  131.3 37.2 %collective-permute-done.4.refs_7_ = bf16[512,384]{1,0:T(8,128)(2,1)S(1)} collective-permute-done((bf16[512,384]{1,0:T(8,128)(2,1)}, bf16[512,384]{1,0:T(8,128)(2,1)S(1)}, u32[]{:S(2)}, u32[]{:S(2)}) %collective-permute-start.4) | collective-permute-done | bytes 393248 | tf_op jit(solution)/shard_map/ppermute | solution.py:185
  171.4 1.3 copy-done.6
  172.8 1.3 copy-done.9
  174.1 1.1 copy-done.17
  176.3 1.1 copy-done.21
  178.5 6.3 %shard_map.49 = (bf16[1024,512]{1,0:T(8,128)(2,1)S(1)}, bf16[1024,512]{1,0:T(8,128)(2,1)S(1)}, bf16[512,640]{1,0:T(8,128)(2,1)S(1)}, bf16[512,640]{1,0:T(8,128)(...) custom-call(s32[2]{0:T(128)S(1)} %pad_add_fusion.place_ref, ...), custom_call_target="tpu_custom_call", output_to_operand_aliasing={{6}: (11, {})} | custom-call | tf_op jit(solution)/shard_map/pallas_call | solution.py:115
  190.9 8.4 %all-to-all-start.3 = ((bf16[32,24,512]{2,1,0:T(8,128)(2,1)}), bf16[32,24,512]{2,1,0:T(8,128)(2,1)}, u32[]{:S(2)}, u32[]{:S(2)}) async-start(bf16[32,24,512]{2,1,0:T(8,128)(2,1)} %bitcast.22), calls=%async_computation.3 | async-start | bytes 1572864 | tf_op jit(solution)/shard_map/all_to_all | solution.py:193
  199.5 2.3 collective-permute-start.7
  203.5 2.7 collective-permute-start.10
  206.2 15.1 %collective-permute-done.10.refs_10_ = bf16[256,768]{1,0:T(8,128)(2,1)S(1)} collective-permute-done((bf16[256,768]{1,0:T(8,128)(2,1)}, bf16[256,768]{1,0:T(8,128)(2,1)S(1)}, u32[]{:S(2)}, u32[]{:S(2)}) %collective-permute-start.10) | collective-permute-done | bytes 393248 | tf_op jit(solution)/shard_map/ppermute | solution.py:187
  221.3 18.9 %collective-permute-done.8.refs_7_ = bf16[512,640]{1,0:T(8,128)(2,1)S(1)} collective-permute-done((bf16[512,640]{1,0:T(8,128)(2,1)}, bf16[512,640]{1,0:T(8,128)(2,1)S(1)}, u32[]{:S(2)}, u32[]{:S(2)}) %collective-permute-start.8) | collective-permute-done | bytes 655392 | tf_op jit(solution)/shard_map/ppermute | solution.py:185
  243.9 1.3 copy-done.7
  245.2 1.3 copy-done.10
  246.5 1.2 copy-done.12
  247.8 1.2 copy-done.14
  252.3 5.6 %shard_map.50 = (bf16[1024,256]{1,0:T(8,128)(2,1)S(1)}, bf16[1024,256]{1,0:T(8,128)(2,1)S(1)}, bf16[512,512]{1,0:T(8,128)(2,1)S(1)}, bf16[512,512]{1,0:T(8,128)(...) custom-call(s32[2]{0:T(128)S(1)} %pad_add_fusion.place_ref, ...), custom_call_target="tpu_custom_call" | custom-call | tf_op jit(solution)/shard_map/pallas_call | solution.py:115
  257.9 2.8 collective-permute-start.15
  261.1 2.2 collective-permute-start.12
  264.8 10.8 %collective-permute-done.11.refs_1_ = bf16[1024,256]{1,0:T(8,128)(2,1)S(1)} collective-permute-done((bf16[1024,256]{1,0:T(8,128)(2,1)S(1)}, bf16[1024,256]{1,0:T(8,128)(2,1)S(1)}, u32[]{:S(2)}, u32[]{:S(2)}) %collective-permute-start.11) | collective-permute-done | bytes 524320 | tf_op jit(solution)/shard_map/ppermute | solution.py:183
  275.6 1.6 collective-permute-done.12.refs_2_
  277.2 8.8 %collective-permute-done.13.refs_6_ = bf16[512,512]{1,0:T(8,128)(2,1)S(1)} collective-permute-done((bf16[512,512]{1,0:T(8,128)(2,1)S(1)}, bf16[512,512]{1,0:T(8,128)(2,1)S(1)}, u32[]{:S(2)}, u32[]{:S(2)}) %collective-permute-start.13) | collective-permute-done | bytes 524320 | tf_op jit(solution)/shard_map/ppermute | solution.py:185
  286.0 3.5 %shard_map.51 = (bf16[512,256]{1,0:T(8,128)(2,1)S(1)}, bf16[512,256]{1,0:T(8,128)(2,1)S(1)}, bf16[256,1024]{1,0:T(8,128)(2,1)S(1)}, f32[256,1024]{1,0:T(8,128)S(1)}, bf16[256,1280]{1,0:T(8,128)(2,1)S(1)}) custom-call(s32[2]{0:T(128)S(1)} %pad_add_fusion.place_ref, bf16[768,2048]{1,0:T(8,128)(2,1)S(1)} %bitcast.17, bf16[768,512]{1,0:T(8,128)(2,1)} %bitcast.12.refs_0_, ...), custom_call_target="tpu_custom_call" | custom-call | tf_op jit(solution)/shard_map/pallas_call | solution.py:115
  290.4 2.2 collective-permute-start.16
  292.7 5.3 %collective-permute-done.16.refs_3_ = bf16[512,256]{1,0:T(8,128)(2,1)S(1)} collective-permute-done((bf16[512,256]{1,0:T(8,128)(2,1)S(1)}, bf16[512,256]{1,0:T(8,128)(2,1)S(1)}, u32[]{:S(2)}, u32[]{:S(2)}) %collective-permute-start.16) | collective-permute-done | bytes 262176 | tf_op jit(solution)/shard_map/ppermute | solution.py:185
  299.0 3.6 %collective-permute-done.18.refs_6_ = bf16[256,1024]{1,0:T(8,128)(2,1)S(1)} collective-permute-done((bf16[256,1024]{1,0:T(8,128)(2,1)S(1)}, bf16[256,1024]{1,0:T(8,128)(2,1)S(1)}, u32[]{:S(2)}, u32[]{:S(2)}) %collective-permute-start.18) | collective-permute-done | bytes 524320 | tf_op jit(solution)/shard_map/ppermute | solution.py:187
  302.7 2.1 shard_map.52
  305.6 7.1 %collective-permute-done.19.refs_1_ = bf16[256,512]{1,0:T(8,128)(2,1)S(1)} collective-permute-done((bf16[256,512]{1,0:T(8,128)(2,1)S(1)}, bf16[256,512]{1,0:T(8,128)(2,1)S(1)}, u32[]{:S(2)}, u32[]{:S(2)}) %collective-permute-start.19) | collective-permute-done | bytes 262176 | tf_op jit(solution)/shard_map/ppermute | solution.py:187
  313.3 1.4 pad_maximum_fusion
  (94 shorter events, 33.8 us)
Async XLA Ops:
  0.0 45.4 %copy-start = (bf16[1,768,2048]{2,1,0:T(8,128)(2,1)S(1)}, bf16[1,768,2048]{2,1,0:T(8,128)(2,1)}, u32[]{:S(2)}) copy-start(bf16[1,768,2048]{2,1,0:T(8,128)(2,1)} %param.7) | copy-start | bytes 9437188
  4.8 40.6 %all-to-all-start = ((bf16[32,24,768]{2,1,0:T(8,128)(2,1)}), bf16[32,24,768]{2,1,0:T(8,128)(2,1)}, u32[]{:S(2)}, u32[]{:S(2)}) async-start(bf16[32,24,768]{2,1,0:T(8,128)(2,1)} %bitcast.23), calls=%async_computation | async-start | bytes 2359296 | tf_op jit(solution)/shard_map/all_to_all | solution.py:193
  45.4 1.5 copy-start.1
  50.1 1.3 copy-start.2
  53.2 53.5 %all-to-all-start.1 = ((bf16[32,24,1280]{2,1,0:T(8,128)(2,1)}), bf16[32,24,1280]{2,1,0:T(8,128)(2,1)}, u32[]{:S(2)}, u32[]{:S(2)}) async-start(bf16[32,24,1280]{2,1,0:T(8,128)(2,1)} %bitcast.20), calls=%async_computation.1 | async-start | bytes 3932160 | tf_op jit(solution)/shard_map/all_to_all | solution.py:193
  58.9 19.9 %collective-permute-start = (bf16[1024,384]{1,0:T(8,128)(2,1)}, bf16[1024,384]{1,0:T(8,128)(2,1)S(1)}, u32[]{:S(2)}, u32[]{:S(2)}) collective-permute-start(bf16[1024,384]{1,0:T(8,128)(2,1)} %copy-done.36), channel_id=1, source_target_pairs={{0,2},{1,3},{2,0},{3,1},{4,6},{5,7},{6,4},{7,5},{8,10},{9,11},{10,... | collective-permute-start | bytes 2359304 | tf_op jit(solution)/shard_map/ppermute | solution.py:183
  60.5 20.7 %collective-permute-start.1 = (bf16[1024,384]{1,0:T(8,128)(2,1)}, bf16[1024,384]{1,0:T(8,128)(2,1)S(1)}, u32[]{:S(2)}, u32[]{:S(2)}) collective-permute-start(bf16[1024,384]{1,0:T(8,128)(2,1)} %copy-done.35), channel_id=1, source_target_pairs={{0,6},{1,7},{2,4},{3,5},{4,2},{5,3},{6,0},{7,1},{8,14},{9,15},{10,... | collective-permute-start | bytes 2359304 | tf_op jit(solution)/shard_map/ppermute | solution.py:183
  106.7 1.4 copy-start.3
  108.1 1.1 copy-start.16
  109.3 1.1 copy-start.19
  115.8 1.1 copy-start.4
  116.9 1.1 copy-start.31
  118.0 1.1 copy-start.32
  120.6 50.8 %all-to-all-start.2 = ((bf16[32,24,1024]{2,1,0:T(8,128)(2,1)}), bf16[32,24,1024]{2,1,0:T(8,128)(2,1)}, u32[]{:S(2)}, u32[]{:S(2)}) async-start(bf16[32,24,1024]{2,1,0:T(8,128)(2,1)} %bitcast.21), calls=%async_computation.2 | async-start | bytes 3145728 | tf_op jit(solution)/shard_map/all_to_all | solution.py:193
  126.4 42.8 %collective-permute-start.2 = (bf16[1024,640]{1,0:T(8,128)(2,1)}, bf16[1024,640]{1,0:T(8,128)(2,1)S(1)}, u32[]{:S(2)}, u32[]{:S(2)}) collective-permute-start(bf16[1024,640]{1,0:T(8,128)(2,1)} %copy-done.32), channel_id=1, source_target_pairs={{0,2},{1,3},{2,0},{3,1},{4,6},{5,7},{6,4},{7,5},{8,10},{9,11},{10,... | collective-permute-start | bytes 3932168 | tf_op jit(solution)/shard_map/ppermute | solution.py:183
  128.0 42.3 %collective-permute-start.3 = (bf16[1024,640]{1,0:T(8,128)(2,1)}, bf16[1024,640]{1,0:T(8,128)(2,1)S(1)}, u32[]{:S(2)}, u32[]{:S(2)}) collective-permute-start(bf16[1024,640]{1,0:T(8,128)(2,1)} %copy-done.31), channel_id=1, source_target_pairs={{0,6},{1,7},{2,4},{3,5},{4,2},{5,3},{6,0},{7,1},{8,14},{9,15},{10,... | collective-permute-start | bytes 3932168 | tf_op jit(solution)/shard_map/ppermute | solution.py:183
  130.2 38.2 %collective-permute-start.4 = (bf16[512,384]{1,0:T(8,128)(2,1)}, bf16[512,384]{1,0:T(8,128)(2,1)S(1)}, u32[]{:S(2)}, u32[]{:S(2)}) collective-permute-start(bf16[512,384]{1,0:T(8,128)(2,1)} %copy-done.41), channel_id=1, source_target_pairs={{0,6},{1,7},{2,4},{3,5},{4,2},{5,3},{6,0},{7,1},{8,14},{9,15},{10,... | collective-permute-start | bytes 1179656 | tf_op jit(solution)/shard_map/ppermute | solution.py:185
  131.3 37.2 %collective-permute-start.5 = (bf16[512,384]{1,0:T(8,128)(2,1)}, bf16[512,384]{1,0:T(8,128)(2,1)S(1)}, u32[]{:S(2)}, u32[]{:S(2)}) collective-permute-start(bf16[512,384]{1,0:T(8,128)(2,1)} %copy-done.40), channel_id=1, source_target_pairs={{0,2},{1,3},{2,0},{3,1},{4,6},{5,7},{6,4},{7,5},{8,10},{9,11},{10,... | collective-permute-start | bytes 1179656 | tf_op jit(solution)/shard_map/ppermute | solution.py:185
  169.2 1.1 copy-start.5
  170.3 1.1 copy-start.8
  171.4 1.3 copy-start.6
  172.8 1.3 copy-start.9
  174.1 1.1 copy-start.17
  175.2 1.1 copy-start.20
  176.3 1.1 copy-start.21
  177.5 1.0 copy-start.30
  190.9 52.9 %all-to-all-start.3 = ((bf16[32,24,512]{2,1,0:T(8,128)(2,1)}), bf16[32,24,512]{2,1,0:T(8,128)(2,1)}, u32[]{:S(2)}, u32[]{:S(2)}) async-start(bf16[32,24,512]{2,1,0:T(8,128)(2,1)} %bitcast.22), calls=%async_computation.3 | async-start | bytes 1572864 | tf_op jit(solution)/shard_map/all_to_all | solution.py:193
  199.4 42.6 %collective-permute-start.6 = (bf16[1024,512]{1,0:T(8,128)(2,1)}, bf16[1024,512]{1,0:T(8,128)(2,1)S(1)}, u32[]{:S(2)}, u32[]{:S(2)}) collective-permute-start(bf16[1024,512]{1,0:T(8,128)(2,1)} %copy-done.34), channel_id=1, source_target_pairs={{0,2},{1,3},{2,0},{3,1},{4,6},{5,7},{6,4},{7,5},{8,10},{9,11},{10,... | collective-permute-start | bytes 3145736 | tf_op jit(solution)/shard_map/ppermute | solution.py:183
  199.5 43.4 %collective-permute-start.7 = (bf16[1024,512]{1,0:T(8,128)(2,1)}, bf16[1024,512]{1,0:T(8,128)(2,1)S(1)}, u32[]{:S(2)}, u32[]{:S(2)}) collective-permute-start(bf16[1024,512]{1,0:T(8,128)(2,1)} %copy-done.33), channel_id=1, source_target_pairs={{0,6},{1,7},{2,4},{3,5},{4,2},{5,3},{6,0},{7,1},{8,14},{9,15},{10,... | collective-permute-start | bytes 3145736 | tf_op jit(solution)/shard_map/ppermute | solution.py:183
  201.8 38.5 %collective-permute-start.8 = (bf16[512,640]{1,0:T(8,128)(2,1)}, bf16[512,640]{1,0:T(8,128)(2,1)S(1)}, u32[]{:S(2)}, u32[]{:S(2)}) collective-permute-start(bf16[512,640]{1,0:T(8,128)(2,1)} %copy-done.38), channel_id=1, source_target_pairs={{0,6},{1,7},{2,4},{3,5},{4,2},{5,3},{6,0},{7,1},{8,14},{9,15},{10,... | collective-permute-start | bytes 1966088 | tf_op jit(solution)/shard_map/ppermute | solution.py:185
  202.8 38.3 %collective-permute-start.9 = (bf16[512,640]{1,0:T(8,128)(2,1)}, bf16[512,640]{1,0:T(8,128)(2,1)S(1)}, u32[]{:S(2)}, u32[]{:S(2)}) collective-permute-start(bf16[512,640]{1,0:T(8,128)(2,1)} %copy-done.37), channel_id=1, source_target_pairs={{0,2},{1,3},{2,0},{3,1},{4,6},{5,7},{6,4},{7,5},{8,10},{9,11},{10,... | collective-permute-start | bytes 1966088 | tf_op jit(solution)/shard_map/ppermute | solution.py:185
  203.5 17.8 %collective-permute-start.10 = (bf16[256,768]{1,0:T(8,128)(2,1)}, bf16[256,768]{1,0:T(8,128)(2,1)S(1)}, u32[]{:S(2)}, u32[]{:S(2)}) collective-permute-start(bf16[256,768]{1,0:T(8,128)(2,1)} %copy-done.39), channel_id=1, source_target_pairs={{0,1},{1,0},{2,3},{3,2},{4,5},{5,4},{6,7},{7,6},{8,9},{9,8},{10,11... | collective-permute-start | bytes 1179656 | tf_op jit(solution)/shard_map/ppermute | solution.py:187
  243.9 1.3 copy-start.7
  245.2 1.3 copy-start.10
  246.5 1.2 copy-start.12
  247.8 1.2 copy-start.14
  249.0 1.1 copy-start.24
  250.1 1.1 copy-start.26
  251.2 1.1 copy-start.28
  257.9 28.2 %collective-permute-start.15 = (bf16[256,1280]{1,0:T(8,128)(2,1)S(1)}, bf16[256,1280]{1,0:T(8,128)(2,1)S(1)}, u32[]{:S(2)}, u32[]{:S(2)}) collective-permute-start(bf16[256,1280]{1,0:T(8,128)(2,1)S(1)} %get-tuple-element.64), channel_id=1, source_target_pairs={{0,1},{1,0},{2,3},{3,2},{4,5},{5,4},{6,7},{7,6},{8,9},{9,8},{10,11... | collective-permute-start | bytes 1966088 | tf_op jit(solution)/shard_map/ppermute | solution.py:187
  260.7 14.9 %collective-permute-start.11 = (bf16[1024,256]{1,0:T(8,128)(2,1)S(1)}, bf16[1024,256]{1,0:T(8,128)(2,1)S(1)}, u32[]{:S(2)}, u32[]{:S(2)}) collective-permute-start(bf16[1024,256]{1,0:T(8,128)(2,1)S(1)} %get-tuple-element.59), channel_id=1, source_target_pairs={{0,2},{1,3},{2,0},{3,1},{4,6},{5,7},{6,4},{7,5},{8,10},{9,11},{10,... | collective-permute-start | bytes 1572872 | tf_op jit(solution)/shard_map/ppermute | solution.py:183
  261.1 16.1 %collective-permute-start.12 = (bf16[1024,256]{1,0:T(8,128)(2,1)S(1)}, bf16[1024,256]{1,0:T(8,128)(2,1)S(1)}, u32[]{:S(2)}, u32[]{:S(2)}) collective-permute-start(bf16[1024,256]{1,0:T(8,128)(2,1)S(1)} %get-tuple-element.60), channel_id=1, source_target_pairs={{0,6},{1,7},{2,4},{3,5},{4,2},{5,3},{6,0},{7,1},{8,14},{9,15},{10,... | collective-permute-start | bytes 1572872 | tf_op jit(solution)/shard_map/ppermute | solution.py:183
  263.3 22.7 %collective-permute-start.13 = (bf16[512,512]{1,0:T(8,128)(2,1)S(1)}, bf16[512,512]{1,0:T(8,128)(2,1)S(1)}, u32[]{:S(2)}, u32[]{:S(2)}) collective-permute-start(bf16[512,512]{1,0:T(8,128)(2,1)S(1)} %get-tuple-element.61), channel_id=1, source_target_pairs={{0,6},{1,7},{2,4},{3,5},{4,2},{5,3},{6,0},{7,1},{8,14},{9,15},{10,... | collective-permute-start | bytes 1572872 | tf_op jit(solution)/shard_map/ppermute | solution.py:185
  264.4 21.6 %collective-permute-start.14 = (bf16[512,512]{1,0:T(8,128)(2,1)S(1)}, bf16[512,512]{1,0:T(8,128)(2,1)S(1)}, u32[]{:S(2)}, u32[]{:S(2)}) collective-permute-start(bf16[512,512]{1,0:T(8,128)(2,1)S(1)} %get-tuple-element.62), channel_id=1, source_target_pairs={{0,2},{1,3},{2,0},{3,1},{4,6},{5,7},{6,4},{7,5},{8,10},{9,11},{10,... | collective-permute-start | bytes 1572872 | tf_op jit(solution)/shard_map/ppermute | solution.py:185
  289.6 13.1 %collective-permute-start.18 = (bf16[256,1024]{1,0:T(8,128)(2,1)S(1)}, bf16[256,1024]{1,0:T(8,128)(2,1)S(1)}, u32[]{:S(2)}, u32[]{:S(2)}) collective-permute-start(bf16[256,1024]{1,0:T(8,128)(2,1)S(1)} %get-tuple-element.69), channel_id=1, source_target_pairs={{0,1},{1,0},{2,3},{3,2},{4,5},{5,4},{6,7},{7,6},{8,9},{9,8},{10,11... | collective-permute-start | bytes 1572872 | tf_op jit(solution)/shard_map/ppermute | solution.py:187
  290.4 7.6 %collective-permute-start.16 = (bf16[512,256]{1,0:T(8,128)(2,1)S(1)}, bf16[512,256]{1,0:T(8,128)(2,1)S(1)}, u32[]{:S(2)}, u32[]{:S(2)}) collective-permute-start(bf16[512,256]{1,0:T(8,128)(2,1)S(1)} %get-tuple-element.66), channel_id=1, source_target_pairs={{0,6},{1,7},{2,4},{3,5},{4,2},{5,3},{6,0},{7,1},{8,14},{9,15},{10,... | collective-permute-start | bytes 786440 | tf_op jit(solution)/shard_map/ppermute | solution.py:185
  292.7 6.4 %collective-permute-start.17 = (bf16[512,256]{1,0:T(8,128)(2,1)S(1)}, bf16[512,256]{1,0:T(8,128)(2,1)S(1)}, u32[]{:S(2)}, u32[]{:S(2)}) collective-permute-start(bf16[512,256]{1,0:T(8,128)(2,1)S(1)} %get-tuple-element.67), channel_id=1, source_target_pairs={{0,2},{1,3},{2,0},{3,1},{4,6},{5,7},{6,4},{7,5},{8,10},{9,11},{10,... | collective-permute-start | bytes 786440 | tf_op jit(solution)/shard_map/ppermute | solution.py:185
  304.7 8.0 %collective-permute-start.19 = (bf16[256,512]{1,0:T(8,128)(2,1)S(1)}, bf16[256,512]{1,0:T(8,128)(2,1)S(1)}, u32[]{:S(2)}, u32[]{:S(2)}) collective-permute-start(bf16[256,512]{1,0:T(8,128)(2,1)S(1)} %get-tuple-element.72), channel_id=1, source_target_pairs={{0,1},{1,0},{2,3},{3,2},{4,5},{5,4},{6,7},{7,6},{8,9},{9,8},{10,11... | collective-permute-start | bytes 786440 | tf_op jit(solution)/shard_map/ppermute | solution.py:187
  (18 other events, 15.7 us)

commit v3 on v1

v3 whole, which is shorter than its diff:
```python
import functools

import jax
import jax.numpy as jnp
from jax import lax
from jax.experimental import pallas as pl
from jax.experimental.pallas import tpu as pltpu
from jax.sharding import PartitionSpec as P

EXP_DEV = 4
TWO = ((0, 1, 2), (1, 0, 2))
THREE = ((0, 1, 2), (1, 2, 0), (2, 0, 1))
WIDTHS = ((512, 512), (768, 768), (384, 384, 256))
ORDERS = (TWO, TWO, THREE)
VMEM = 16 * 1024 * 1024
STEPS = (
    ((0, 0),),
    ((0, 1),),
    ((1, 0),),
    ((2, 0),),
    ((3, 0),),
    ((0, 2),),
    ((1, 1),),
    ((2, 1), (4, 0)),
    ((1, 2),),
    ((3, 1),),
    ((2, 2), (4, 1)),
    ((3, 2),),
    ((4, 2),),
)


def rows_kernel(columns, capacity, start, routes_ref, probs_ref, grad_ref, token_ref, out_ref, _):
    top, tok = routes_ref.shape
    ids = lax.broadcasted_iota(jnp.int32, (columns, tok), 0) * EXP_DEV
    named = jnp.zeros((columns, tok), jnp.float32)
    prob = jnp.zeros((columns, tok), jnp.float32)
    for k in range(top):
        hit = routes_ref[k : k + 1, :] == ids
        named = named + jnp.where(hit, 1.0, 0.0)
        prob = prob + jnp.where(hit, probs_ref[k : k + 1, :], 0.0)
    row = lax.broadcasted_iota(jnp.int32, (tok, tok), 0)
    col = lax.broadcasted_iota(jnp.int32, (tok, tok), 1)
    earlier = jnp.where(row < col, 1.0, 0.0).astype(jnp.bfloat16)
    slot = jnp.dot(named.astype(jnp.bfloat16), earlier, preferred_element_type=jnp.float32)
    slot = jnp.where(named > 0.0, slot, -1.0).astype(jnp.int32)
    places = lax.broadcasted_iota(jnp.int32, (columns, capacity, tok), 1)
    pick = slot[:, None, :] == places
    weight = jnp.sum(jnp.where(pick, prob[:, None, :], 0.0), axis=2, keepdims=True)
    weight = weight.reshape(columns * capacity, 1)
    pick = jnp.where(pick, 1.0, 0.0).reshape(columns * capacity, tok).astype(jnp.bfloat16)
    width = out_ref.shape[1]
    taken = jnp.dot(pick, grad_ref[:, start : start + width], preferred_element_type=jnp.float32)
    out_ref[...] = (weight * taken).astype(jnp.bfloat16)


def block_of(place_ref, order, bits):
    y, xh = place_ref[0], place_ref[1]
    for kind, bit in zip(order, bits):
        if bit:
            y, xh = (y ^ 1, xh) if kind == 0 else (3 - y, xh) if kind == 1 else (y, 1 - xh)
    return y * 2 + xh


def product(place_ref, hidden_ref, size, order, bits, rows):
    at = pl.multiple_of(block_of(place_ref, order, bits) * size, size)
    return lax.dot_general(
        hidden_ref[:, pl.ds(at, size)],
        rows,
        (((0,), (0,)), ((), ())),
        preferred_element_type=jnp.float32,
    )


def terms(kind, orders, size, place_ref, hidden_ref, ins, outs):
    arrived_ref, came = ins[0], ins[1:]
    start = 0
    for part, order in enumerate(orders):
        width = outs[part].shape[1]
        rows = arrived_ref[:, start : start + width]
        start += width
        earlier = [came[e * len(orders) + part] for e in range(kind - 1)]
        if kind == 1:
            targets = [(outs[part], (1, i, j)) for i in (1, 0) for j in (1, 0)]
        elif kind == 2:
            targets = [(outs[part], (0, 1, j)) for j in (1, 0)]
        else:
            targets = [(outs[part], (0, 0, 1)), (outs[len(orders) + part], (0, 0, 0))]
        filled = {}
        for out_ref, bits in targets:
            total = product(place_ref, hidden_ref, size, order, bits, rows)
            if kind > 1:
                at = (2 * (1 - bits[1]) + 1 - bits[2]) * size
                total = total + earlier[0][at : at + size, :].astype(jnp.float32)
            if kind > 2:
                at = (1 - bits[2]) * size
                total = total + earlier[1][at : at + size, :].astype(jnp.float32)
            at = filled.get(id(out_ref), 0)
            out_ref[at : at + size, :] = total.astype(out_ref.dtype)
            filled[id(out_ref)] = at + size


def last_sum(ins, outs):
    start = 0
    parts = len(ins) // 2
    for part in range(parts):
        width = ins[part].shape[1]
        total = ins[part][...] + ins[parts + part][...].astype(jnp.float32)
        outs[0][:, start : start + width] = total.astype(jnp.bfloat16)
        start += width


def step_kernel(size, jobs, place_ref, hidden_ref, *refs):
    ins = refs[: sum(n for _, _, n, _ in jobs)]
    outs = refs[len(ins) + 1 :]
    i = o = 0
    for kind, orders, n_in, n_out in jobs:
        if kind == 4:
            last_sum(ins[i : i + n_in], outs[o : o + n_out])
        else:
            terms(kind, orders, size, place_ref, hidden_ref, ins[i : i + n_in], outs[o : o + n_out])
        i, o = i + n_in, o + n_out


def step(size, place, hidden, token, jobs):
    ins = [x for _, _, given, _ in jobs for x in given]
    shapes = [s for _, _, _, made in jobs for s in made]
    counts = [(kind, orders, len(given), len(made)) for kind, orders, given, made in jobs]
    vmem, anywhere = pl.BlockSpec(memory_space=pltpu.VMEM), pl.BlockSpec(memory_space=pl.ANY)
    res = pl.pallas_call(
        functools.partial(step_kernel, size, counts),
        in_specs=[pl.BlockSpec(memory_space=pltpu.SMEM), vmem] + [vmem] * len(ins) + [anywhere],
        out_specs=[vmem] * len(shapes) + [anywhere],
        out_shape=shapes + [jax.ShapeDtypeStruct(token.shape, token.dtype)],
        input_output_aliases={2 + len(ins): len(shapes)},
        compiler_params=pltpu.CompilerParams(vmem_limit_bytes=VMEM),
    )(place, hidden, *ins, token)
    made, at = [], 0
    for _, _, _, n_out in counts:
        made.append(res[at : at + n_out])
        at += n_out
    return made, res[-1]


def shards(grad_out, route_probs, routes, hidden_saved):
    tok, model_cols = grad_out.shape
    flight, slot_count, hidden = hidden_saved.shape
    ranks = lax.axis_size("ep")
    peers = lax.axis_size("dp")
    capacity = slot_count // ranks
    size = hidden // peers
    dp = lax.axis_index("dp")
    place = jnp.stack([dp // 2, dp % 2]).astype(jnp.int32)
    token = jnp.zeros((8, 128), jnp.int32)
    vmem, anywhere = pl.BlockSpec(memory_space=pltpu.VMEM), pl.BlockSpec(memory_space=pl.ANY)
    partners = (
        [(i, i ^ 2) for i in range(peers)],
        [(i, (3 - i // 2) * 2 + i % 2) for i in range(peers)],
        [(i, i ^ 1) for i in range(peers)],
    )

    def shape(rows, cols, dtype=jnp.bfloat16):
        return jax.ShapeDtypeStruct((rows, cols), dtype)

    arrived, came, keep, out = {}, {}, {}, {}
    for names in STEPS:
        if names[0][0] == 0:
            c = names[0][1]
            width = sum(WIDTHS[c])
            start = sum(sum(w) for w in WIDTHS[:c])
            rows, token = pl.pallas_call(
                functools.partial(rows_kernel, ranks, capacity, start),
                in_specs=[vmem] * 3 + [anywhere],
                out_specs=[vmem, anywhere],
                out_shape=[shape(slot_count, width), jax.ShapeDtypeStruct(token.shape, token.dtype)],
                input_output_aliases={3: 1},
                compiler_params=pltpu.CompilerParams(vmem_limit_bytes=VMEM),
            )(routes.T, route_probs.T, grad_out, token)
            rows = rows.reshape(ranks, capacity, width)
            rows = lax.all_to_all(rows, "ep", split_axis=0, concat_axis=0, tiled=True)
            arrived[c], came[c] = rows.reshape(slot_count, width), []
            continue
        jobs = []
        for kind, c in names:
            if kind == 4:
                jobs.append((4, ORDERS[c], keep[c] + came[c][2 * len(ORDERS[c]) :], [shape(size, sum(WIDTHS[c]))]))
                continue
            made = [shape(hidden >> kind, w) for w in WIDTHS[c]]
            if kind == 3:
                made += [shape(size, w, jnp.float32) for w in WIDTHS[c]]
            jobs.append((kind, ORDERS[c], [arrived[c]] + came[c], made))
        results, token = step(size, place, hidden_saved[0], token, jobs)
        for (kind, c), made in zip(names, results):
            if kind == 4:
                out[c] = made[0]
                continue
            came[c] = came[c] + [
                lax.ppermute(m, "dp", partners[order[kind - 1]]) for m, order in zip(made, ORDERS[c])
            ]
            keep[c] = list(made[len(ORDERS[c]) :])
    return jnp.concatenate([out[c] for c in range(len(WIDTHS))], axis=1)


def solution(mesh):
    in_specs = (
        P(("ep", "dp"), None),
        P(("ep", "dp"), None),
        P(("ep", "dp"), None),
        P(("ep", "dp"), None, None),
    )
    return jax.shard_map(
        shards, mesh=mesh, in_specs=in_specs, out_specs=P("dp", "ep"), check_vma=False
    )
```

time: 449 us -> 243 us (0.54)
  blocking collectives: 165 us -> 0 us
  waiting for transfers between devices: 237 us -> 142 us
  starting transfers between devices: 0.13 us -> 55 us
  Pallas kernels: 3.31 us -> 31.1 us
  matrix products: 18.2 us -> 0 us
  between operations: 13.2 us -> 0.25 us
    reduce_scatter x4 -> x0, waiting for transfers between devices: 237 us -> none  [shards(): parts.append(lax.psum_scatter(term, 'dp', scatter_dimension=0, tiled=True))]
    all_to_all x4 -> x0, blocking collectives: 165 us -> none  [shards(): lax.all_to_all(rows, 'ep', split_axis=0, concat_axis=0, tiled=True)]
    ppermute x0 -> x21, waiting for transfers between devices: none -> 103 us  [shards(): lax.ppermute(m, 'dp', partners[order[kind - 1]])]
    all_to_all x0 -> x3, waiting for transfers between devices: none -> 38.9 us  [shards(): rows = lax.all_to_all(rows, 'ep', split_axis=0, concat_axis=0, tiled=True)]
    ppermute x0 -> x21, starting transfers between devices: none -> 33.8 us  [shards(): lax.ppermute(m, 'dp', partners[order[kind - 1]])]
    pallas_call x1 -> x13, Pallas kernels: 3.31 us -> 31.1 us  [the longest x10 28.6 us: step(): pl.pallas_call(functools.partial(step_kernel, size, counts), in_specs=[pl...]
    all_to_all x0 -> x3, starting transfers between devices: none -> 21.3 us  [shards(): rows = lax.all_to_all(rows, 'ep', split_axis=0, concat_axis=0, tiled=True)]
    dot_general x4 -> x0, matrix products: 18.2 us -> none  [expert_term(): lax.dot_general(hidden_rows, arrived, (((0,), (0,)), ((), ())), preferred...]
  transfers between devices with their start and end apart: 4 -> 24, of which waited for: 3 -> 17; matrix products, arithmetic and copies ran while one was open for 3% -> 0% of each run, Pallas kernels for 0% -> 10%
where the time goes in v3:
time: 243 us
  waiting for transfers between devices  142 us (58%)
  starting transfers between devices  55 us (23%)
  Pallas kernels  31.1 us (13%)
  local copies, waits for them, and re-layouts  12.6 us (5%)
    ppermute x21, waiting for transfers between devices, shards(): lax.ppermute(m, 'dp', partners[order[kind - 1]])  103 us
    all_to_all x3, waiting for transfers between devices, shards(): rows = lax.all_to_all(rows, 'ep', split_axis=0, concat_axis=0, tiled=True)  38.9 us
    ppermute x21, starting transfers between devices, shards(): lax.ppermute(m, 'dp', partners[order[kind - 1]])  33.8 us
    pallas_call x10, Pallas kernels, step(): pl.pallas_call(functools.partial(step_kernel, size, counts), in_specs=[pl...  28.6 us
    all_to_all x3, starting transfers between devices, shards(): rows = lax.all_to_all(rows, 'ep', split_axis=0, concat_axis=0, tiled=True)  21.3 us
    unnamed x50, local copies, waits for them, and re-layouts  12.6 us
  transfers between devices with their start and end apart: 24, of which 17 were waited for; matrix products, arithmetic and copies ran while one was open for 0% of the time, Pallas kernels for 10%

profile of v3, /device:TPU:32, one launch (start us, length us, event | category | flops | bytes accessed | tf_op | source)
XLA Modules:
  0.0 242.7 jit_solution(11399706919371714255)
XLA Ops:
  0.0 1.3 copy-done.3
  3.5 1.1 copy-done.12
  4.6 9.8 %all-to-all-start.1 = ((bf16[32,24,1024]{2,1,0:T(8,128)(2,1)}), bf16[32,24,1024]{2,1,0:T(8,128)(2,1)S(1)}, u32[]{:S(2)}, u32[]{:S(2)}) async-start(bf16[32,24,1024]{2,1,0:T(8,128)(2,1)} %bitcast.26), calls=%async_computation.1 | async-start | bytes 3145728 | tf_op jit(solution)/shard_map/all_to_all | solution.py:180
  15.4 1.5 copy-done.10
  16.9 36.9 %all-to-all-done.1 = bf16[32,24,1024]{2,1,0:T(8,128)(2,1)S(1)} async-done(((bf16[32,24,1024]{2,1,0:T(8,128)(2,1)}), bf16[32,24,1024]{2,1,0:T(8,128)(2,1)S(1)}, u32[]{:S(2)}, u32[]{:S(2)}) %all-to-all-start.1) | async-done | bytes 1572896 | tf_op jit(solution)/shard_map/all_to_all | solution.py:180
  53.7 1.1 copy-done.1
  54.9 5.1 %all-to-all-start = ((bf16[32,24,1536]{2,1,0:T(8,128)(2,1)}), bf16[32,24,1536]{2,1,0:T(8,128)(2,1)}, u32[]{:S(2)}, u32[]{:S(2)}) async-start(bf16[32,24,1536]{2,1,0:T(8,128)(2,1)} %bitcast.24), calls=%async_computation | async-start | bytes 4718592 | tf_op jit(solution)/shard_map/all_to_all | solution.py:180
  60.0 1.4 copy-done.2
  61.4 2.4 shard_map.48
  63.9 1.7 collective-permute-start
  65.5 2.2 collective-permute-start.1
  67.7 21.5 %collective-permute-done.refs_1_ = bf16[1024,512]{1,0:T(8,128)(2,1)S(1)} collective-permute-done((bf16[1024,512]{1,0:T(8,128)(2,1)S(1)}, bf16[1024,512]{1,0:T(8,128)(2,1)S(1)}, u32[]{:S(2)}, u32[]{:S(2)}) %collective-permute-start) | collective-permute-done | bytes 1048608 | tf_op jit(solution)/shard_map/ppermute | solution.py:198
  89.2 2.5 %collective-permute-done.1.refs_2_ = bf16[1024,512]{1,0:T(8,128)(2,1)S(1)} collective-permute-done((bf16[1024,512]{1,0:T(8,128)(2,1)S(1)}, bf16[1024,512]{1,0:T(8,128)(2,1)S(1)}, u32[]{:S(2)}, u32[]{:S(2)}) %collective-permute-start.1) | collective-permute-done | bytes 1048608 | tf_op jit(solution)/shard_map/ppermute | solution.py:198
  91.7 1.6 shard_map.49
  93.2 2.3 collective-permute-start.2
  95.5 11.9 %collective-permute-done.2.refs_3_ = bf16[512,512]{1,0:T(8,128)(2,1)S(1)} collective-permute-done((bf16[512,512]{1,0:T(8,128)(2,1)S(1)}, bf16[512,512]{1,0:T(8,128)(2,1)S(1)}, u32[]{:S(2)}, u32[]{:S(2)}) %collective-permute-start.2) | collective-permute-done | bytes 524320 | tf_op jit(solution)/shard_map/ppermute | solution.py:198
  108.2 1.7 shard_map.50
  113.1 1.1 copy-done.11
  114.2 2.0 all-to-all-done
  116.2 6.4 %all-to-all-start.2 = ((bf16[32,24,1024]{2,1,0:T(8,128)(2,1)}), bf16[32,24,1024]{2,1,0:T(8,128)(2,1)}, u32[]{:S(2)}, u32[]{:S(2)}) async-start(bf16[32,24,1024]{2,1,0:T(8,128)(2,1)} %bitcast.25), calls=%async_computation.2 | async-start | bytes 3145728 | tf_op jit(solution)/shard_map/all_to_all | solution.py:180
  122.7 4.5 %shard_map.52 = (bf16[1024,768]{1,0:T(8,128)(2,1)S(1)}, bf16[1024,768]{1,0:T(8,128)(2,1)S(1)}, s32[8,128]{1,0:T(8,128)S(1)}) custom-call(s32[2]{0:T(128)S(1)} %pad_add_fusion.place_ref, bf16[768,2048]{1,0:T(8,128)(2,1)S(1)} %bitcast.14, bf16[768,1536]{1,0:T(8,128)(2,1)} %bitcast.6.refs_0_, ...), custom_call_target="tpu_custom_call", output_to_operand_aliasing={{2}: (3, {})} | custom-call | tf_op jit(solution)/shard_map/pallas_call | solution.py:130
  127.1 1.2 collective-permute-start.4
  128.3 2.2 collective-permute-start.5
  130.5 2.7 %collective-permute-start.6 = (bf16[256,512]{1,0:T(8,128)(2,1)S(1)}, bf16[256,512]{1,0:T(8,128)(2,1)S(1)}, u32[]{:S(2)}, u32[]{:S(2)}) collective-permute-start(bf16[256,512]{1,0:T(8,128)(2,1)S(1)} %copy-done.24), channel_id=1, source_target_pairs={{0,1},{1,0},{2,3},{3,2},{4,5},{5,4},{6,7},{7,6},{8,9},{9,8},{10,11... | collective-permute-start | bytes 786440 | tf_op jit(solution)/shard_map/ppermute | solution.py:198
  134.0 12.4 %collective-permute-done.6.refs_5_ = bf16[256,512]{1,0:T(8,128)(2,1)S(1)} collective-permute-done((bf16[256,512]{1,0:T(8,128)(2,1)S(1)}, bf16[256,512]{1,0:T(8,128)(2,1)S(1)}, u32[]{:S(2)}, u32[]{:S(2)}) %collective-permute-start.6) | collective-permute-done | bytes 262176 | tf_op jit(solution)/shard_map/ppermute | solution.py:198
  146.4 9.6 %collective-permute-done.7.refs_6_ = bf16[256,512]{1,0:T(8,128)(2,1)S(1)} collective-permute-done((bf16[256,512]{1,0:T(8,128)(2,1)S(1)}, bf16[256,512]{1,0:T(8,128)(2,1)S(1)}, u32[]{:S(2)}, u32[]{:S(2)}) %collective-permute-start.7) | collective-permute-done | bytes 262176 | tf_op jit(solution)/shard_map/ppermute | solution.py:198
  156.1 7.8 %collective-permute-done.4.refs_1_ = bf16[1024,768]{1,0:T(8,128)(2,1)S(1)} collective-permute-done((bf16[1024,768]{1,0:T(8,128)(2,1)S(1)}, bf16[1024,768]{1,0:T(8,128)(2,1)S(1)}, u32[]{:S(2)}, u32[]{:S(2)}) %collective-permute-start.4) | collective-permute-done | bytes 1572896 | tf_op jit(solution)/shard_map/ppermute | solution.py:198
  163.9 1.8 collective-permute-done.5.refs_2_
  165.7 4.6 %shard_map.53 = (bf16[512,768]{1,0:T(8,128)(2,1)}, bf16[512,768]{1,0:T(8,128)(2,1)}, bf16[256,1024]{1,0:T(8,128)(2,1)S(1)}, s32[8,128]{1,0:T(8,128)S(1)}) custom-call(s32[2]{0:T(128)S(1)} %pad_add_fusion.place_ref, bf16[768,2048]{1,0:T(8,128)(2,1)S(1)} %bitcast.15, bf16[768,1536]{1,0:T(8,128)(2,1)} %bitcast.6.refs_0_, ...), custom_call_target="tpu_custom_call", output_to_operand_aliasing={{3}: (9, {})} | custom-call | tf_op jit(solution)/shard_map/pallas_call | solution.py:130
  171.1 2.2 collective-permute-start.11
  173.3 3.9 %shard_map.54 = (bf16[1024,384]{1,0:T(8,128)(2,1)S(1)}, bf16[1024,384]{1,0:T(8,128)(2,1)S(1)}, bf16[1024,256]{1,0:T(8,128)(2,1)S(1)}, s32[8,128]{1,0:T(8,128)S(1)}) custom-call(s32[2]{0:T(128)S(1)} %pad_add_fusion.place_ref, bf16[768,2048]{1,0:T(8,128)(2,1)S(1)} %bitcast.16, bf16[768,1024]{1,0:T(8,128)(2,1)} %bitcast.10.refs_0_, ...), custom_call_target="tpu_custom_call", output_to_operand_aliasing={{3}: (3, {})} | custom-call | tf_op jit(solution)/shard_map/pallas_call | solution.py:130
  177.2 2.1 collective-permute-start.8
  179.3 1.1 collective-permute-start.9
  180.4 2.7 %collective-permute-start.10 = (bf16[1024,256]{1,0:T(8,128)(2,1)S(1)}, bf16[1024,256]{1,0:T(8,128)(2,1)S(1)}, u32[]{:S(2)}, u32[]{:S(2)}) collective-permute-start(bf16[1024,256]{1,0:T(8,128)(2,1)S(1)} %get-tuple-element.75), channel_id=1, source_target_pairs={{0,1},{1,0},{2,3},{3,2},{4,5},{5,4},{6,7},{7,6},{8,9},{9,8},{10,11... | collective-permute-start | bytes 1572872 | tf_op jit(solution)/shard_map/ppermute | solution.py:198
  183.1 10.0 %collective-permute-done.11.refs_3_ = bf16[512,768]{1,0:T(8,128)(2,1)} collective-permute-done((bf16[512,768]{1,0:T(8,128)(2,1)}, bf16[512,768]{1,0:T(8,128)(2,1)}, u32[]{:S(2)}, u32[]{:S(2)}) %collective-permute-start.11) | collective-permute-done | bytes 786464 | tf_op jit(solution)/shard_map/ppermute | solution.py:198
  194.1 3.6 %shard_map.55 = (bf16[256,768]{1,0:T(8,128)(2,1)S(1)}, bf16[256,768]{1,0:T(8,128)(2,1)S(1)}, f32[256,768]{1,0:T(8,128)S(1)}, f32[256,768]{1,0:T(8,128)S(1)}, s32[8,128]{1,0:T(8,128)S(1)}) custom-call(s32[2]{0:T(128)S(1)} %pad_add_fusion.place_ref, bf16[768,2048]{1,0:T(8,128)(2,1)S(1)} %bitcast.17, ...), custom_call_target="tpu_custom_call", output_to_operand_aliasing={{4}: (7, {})} | custom-call | tf_op jit(solution)/shard_map/pallas_call | solution.py:130
  197.7 2.8 %collective-permute-start.13 = (bf16[256,768]{1,0:T(8,128)(2,1)S(1)}, bf16[256,768]{1,0:T(8,128)(2,1)S(1)}, u32[]{:S(2)}, u32[]{:S(2)}) collective-permute-start(bf16[256,768]{1,0:T(8,128)(2,1)S(1)} %get-tuple-element.81), channel_id=1, source_target_pairs={{0,1},{1,0},{2,3},{3,2},{4,5},{5,4},{6,7},{7,6},{8,9},{9,8},{10,11... | collective-permute-start | bytes 1179656 | tf_op jit(solution)/shard_map/ppermute | solution.py:198
  201.3 8.7 %collective-permute-done.13.refs_6_ = bf16[256,768]{1,0:T(8,128)(2,1)S(1)} collective-permute-done((bf16[256,768]{1,0:T(8,128)(2,1)S(1)}, bf16[256,768]{1,0:T(8,128)(2,1)S(1)}, u32[]{:S(2)}, u32[]{:S(2)}) %collective-permute-start.13) | collective-permute-done | bytes 393248 | tf_op jit(solution)/shard_map/ppermute | solution.py:198
  210.0 4.2 %collective-permute-done.14.refs_7_ = bf16[256,768]{1,0:T(8,128)(2,1)S(1)} collective-permute-done((bf16[256,768]{1,0:T(8,128)(2,1)S(1)}, bf16[256,768]{1,0:T(8,128)(2,1)S(1)}, u32[]{:S(2)}, u32[]{:S(2)}) %collective-permute-start.14) | collective-permute-done | bytes 393248 | tf_op jit(solution)/shard_map/ppermute | solution.py:198
  214.2 2.9 %shard_map.56 = (bf16[512,384]{1,0:T(8,128)(2,1)S(1)}, bf16[512,384]{1,0:T(8,128)(2,1)S(1)}, bf16[512,256]{1,0:T(8,128)(2,1)S(1)}, bf16[256,1536]{1,0:T(8,128)(2,1)S(1)}, s32[8,128]{1,0:T(8,128)S(1)}) custom-call(s32[2]{0:T(128)S(1)} %pad_add_fusion.place_ref, bf16[768,2048]{1,0:T(8,128)(2,1)S(1)} %bitcast.18, ...), custom_call_target="tpu_custom_call", output_to_operand_aliasing={{4}: (10, {})} | custom-call | tf_op jit(solution)/shard_map/pallas_call | solution.py:130
  217.1 2.1 collective-permute-start.15
  219.2 2.7 %collective-permute-start.16 = (bf16[512,384]{1,0:T(8,128)(2,1)S(1)}, bf16[512,384]{1,0:T(8,128)(2,1)S(1)}, u32[]{:S(2)}, u32[]{:S(2)}) collective-permute-start(bf16[512,384]{1,0:T(8,128)(2,1)S(1)} %get-tuple-element.86), channel_id=1, source_target_pairs={{0,1},{1,0},{2,3},{3,2},{4,5},{5,4},{6,7},{7,6},{8,9},{9,8},{10,11... | collective-permute-start | bytes 1179656 | tf_op jit(solution)/shard_map/ppermute | solution.py:198
  222.0 6.4 %collective-permute-done.17.refs_6_ = bf16[512,256]{1,0:T(8,128)(2,1)S(1)} collective-permute-done((bf16[512,256]{1,0:T(8,128)(2,1)S(1)}, bf16[512,256]{1,0:T(8,128)(2,1)S(1)}, u32[]{:S(2)}, u32[]{:S(2)}) %collective-permute-start.17) | collective-permute-done | bytes 262176 | tf_op jit(solution)/shard_map/ppermute | solution.py:198
  228.5 2.8 %shard_map.57 = (bf16[256,384]{1,0:T(8,128)(2,1)S(1)}, bf16[256,384]{1,0:T(8,128)(2,1)S(1)}, bf16[256,256]{1,0:T(8,128)(2,1)S(1)}, f32[256,384]{1,0:T(8,128)S(1)...) custom-call(s32[2]{0:T(128)S(1)} %pad_add_fusion.place_ref, ...), custom_call_target="tpu_custom_call", output_to_operand_aliasing={{6}: (9, {})} | custom-call | tf_op jit(solution)/shard_map/pallas_call | solution.py:130
  231.3 2.8 %collective-permute-start.18 = (bf16[256,384]{1,0:T(8,128)(2,1)S(1)}, bf16[256,384]{1,0:T(8,128)(2,1)S(1)}, u32[]{:S(2)}, u32[]{:S(2)}) collective-permute-start(bf16[256,384]{1,0:T(8,128)(2,1)S(1)} %get-tuple-element.92), channel_id=1, source_target_pairs={{0,1},{1,0},{2,3},{3,2},{4,5},{5,4},{6,7},{7,6},{8,9},{9,8},{10,11... | collective-permute-start | bytes 589832 | tf_op jit(solution)/shard_map/ppermute | solution.py:198
  234.1 1.5 collective-permute-start.20
  235.6 4.7 %collective-permute-done.20.refs_5_ = bf16[256,256]{1,0:T(8,128)(2,1)S(1)} collective-permute-done((bf16[256,256]{1,0:T(8,128)(2,1)S(1)}, bf16[256,256]{1,0:T(8,128)(2,1)S(1)}, u32[]{:S(2)}, u32[]{:S(2)}) %collective-permute-start.20) | collective-permute-done | bytes 131104 | tf_op jit(solution)/shard_map/ppermute | solution.py:198
  241.4 1.3 pad_maximum_fusion
  (66 shorter events, 11.6 us)
Async XLA Ops:
  0.0 1.3 copy-start.3
  1.3 0.7 copy-start.19
  3.5 1.1 copy-start.12
  4.6 9.8 %copy-start.4 = (bf16[192,3584]{1,0:T(8,128)(2,1)S(1)}, bf16[192,3584]{1,0:T(8,128)(2,1)}, u32[]{:S(2)}) copy-start(bf16[192,3584]{1,0:T(8,128)(2,1)} %grad_ref.5) | copy-start | bytes 4128772
  4.6 49.1 %all-to-all-start.1 = ((bf16[32,24,1024]{2,1,0:T(8,128)(2,1)}), bf16[32,24,1024]{2,1,0:T(8,128)(2,1)S(1)}, u32[]{:S(2)}, u32[]{:S(2)}) async-start(bf16[32,24,1024]{2,1,0:T(8,128)(2,1)} %bitcast.26), calls=%async_computation.1 | async-start | bytes 3145728 | tf_op jit(solution)/shard_map/all_to_all | solution.py:180
  15.4 1.5 copy-start.10
  53.7 1.1 copy-start.1
  54.9 5.2 %copy-start = (bf16[1,768,2048]{2,1,0:T(8,128)(2,1)S(1)}, bf16[1,768,2048]{2,1,0:T(8,128)(2,1)}, u32[]{:S(2)}) copy-start(bf16[1,768,2048]{2,1,0:T(8,128)(2,1)} %param.7) | copy-start | bytes 9437188
  54.9 61.4 %all-to-all-start = ((bf16[32,24,1536]{2,1,0:T(8,128)(2,1)}), bf16[32,24,1536]{2,1,0:T(8,128)(2,1)}, u32[]{:S(2)}, u32[]{:S(2)}) async-start(bf16[32,24,1536]{2,1,0:T(8,128)(2,1)} %bitcast.24), calls=%async_computation | async-start | bytes 4718592 | tf_op jit(solution)/shard_map/all_to_all | solution.py:180
  60.0 1.4 copy-start.2
  63.9 25.3 %collective-permute-start = (bf16[1024,512]{1,0:T(8,128)(2,1)S(1)}, bf16[1024,512]{1,0:T(8,128)(2,1)S(1)}, u32[]{:S(2)}, u32[]{:S(2)}) collective-permute-start(bf16[1024,512]{1,0:T(8,128)(2,1)S(1)} %get-tuple-element.55), channel_id=1, source_target_pairs={{0,2},{1,3},{2,0},{3,1},{4,6},{5,7},{6,4},{7,5},{8,10},{9,11},{10,... | collective-permute-start | bytes 3145736 | tf_op jit(solution)/shard_map/ppermute | solution.py:198
  65.5 26.1 %collective-permute-start.1 = (bf16[1024,512]{1,0:T(8,128)(2,1)S(1)}, bf16[1024,512]{1,0:T(8,128)(2,1)S(1)}, u32[]{:S(2)}, u32[]{:S(2)}) collective-permute-start(bf16[1024,512]{1,0:T(8,128)(2,1)S(1)} %get-tuple-element.56), channel_id=1, source_target_pairs={{0,6},{1,7},{2,4},{3,5},{4,2},{5,3},{6,0},{7,1},{8,14},{9,15},{10,... | collective-permute-start | bytes 3145736 | tf_op jit(solution)/shard_map/ppermute | solution.py:198
  93.2 14.2 %collective-permute-start.2 = (bf16[512,512]{1,0:T(8,128)(2,1)S(1)}, bf16[512,512]{1,0:T(8,128)(2,1)S(1)}, u32[]{:S(2)}, u32[]{:S(2)}) collective-permute-start(bf16[512,512]{1,0:T(8,128)(2,1)S(1)} %get-tuple-element.58), channel_id=1, source_target_pairs={{0,6},{1,7},{2,4},{3,5},{4,2},{5,3},{6,0},{7,1},{8,14},{9,15},{10,... | collective-permute-start | bytes 1572872 | tf_op jit(solution)/shard_map/ppermute | solution.py:198
  95.5 12.6 %collective-permute-start.3 = (bf16[512,512]{1,0:T(8,128)(2,1)S(1)}, bf16[512,512]{1,0:T(8,128)(2,1)S(1)}, u32[]{:S(2)}, u32[]{:S(2)}) collective-permute-start(bf16[512,512]{1,0:T(8,128)(2,1)S(1)} %get-tuple-element.59), channel_id=1, source_target_pairs={{0,2},{1,3},{2,0},{3,1},{4,6},{5,7},{6,4},{7,5},{8,10},{9,11},{10,... | collective-permute-start | bytes 1572872 | tf_op jit(solution)/shard_map/ppermute | solution.py:198
  108.2 4.1 %copy-start.5 = (bf16[192,3584]{1,0:T(8,128)(2,1)S(1)}, bf16[192,3584]{1,0:T(8,128)(2,1)}, u32[]{:S(2)}) copy-start(bf16[192,3584]{1,0:T(8,128)(2,1)} %grad_ref.5) | copy-start | bytes 4128772
  108.2 4.1 %copy-start.20 = (s32[192,8]{0,1:T(8,128)S(1)}, s32[192,8]{0,1:T(8,128)}, u32[]{:S(2)}) copy-start(s32[192,8]{0,1:T(8,128)} %param.6) | copy-start | bytes 18436
  108.2 4.1 %copy-start.22 = (f32[192,8]{0,1:T(8,128)S(1)}, f32[192,8]{0,1:T(8,128)}, u32[]{:S(2)}) copy-start(f32[192,8]{0,1:T(8,128)} %param.5) | copy-start | bytes 18436
  109.9 0.9 copy-start.15
  110.7 0.8 copy-start.17
  111.5 0.7 copy-start.23
  113.0 1.1 copy-start.11
  116.2 57.1 %all-to-all-start.2 = ((bf16[32,24,1024]{2,1,0:T(8,128)(2,1)}), bf16[32,24,1024]{2,1,0:T(8,128)(2,1)}, u32[]{:S(2)}, u32[]{:S(2)}) async-start(bf16[32,24,1024]{2,1,0:T(8,128)(2,1)} %bitcast.25), calls=%async_computation.2 | async-start | bytes 3145728 | tf_op jit(solution)/shard_map/all_to_all | solution.py:180
  122.6 7.9 %copy-start.24 = (bf16[256,512]{1,0:T(8,128)(2,1)S(1)}, bf16[256,512]{1,0:T(8,128)(2,1)}, u32[]{:S(2)}) copy-start(bf16[256,512]{1,0:T(8,128)(2,1)} %copy-done.23) | copy-start | bytes 786436
  122.6 43.0 %copy-start.16 = (f32[256,512]{1,0:T(8,128)S(1)}, f32[256,512]{1,0:T(8,128)}, u32[]{:S(2)}) copy-start(f32[256,512]{1,0:T(8,128)} %copy-done.15) | copy-start | bytes 1572868
  122.7 43.0 %copy-start.18 = (f32[256,512]{1,0:T(8,128)S(1)}, f32[256,512]{1,0:T(8,128)}, u32[]{:S(2)}) copy-start(f32[256,512]{1,0:T(8,128)} %copy-done.17) | copy-start | bytes 1572868
  127.1 36.7 %collective-permute-start.4 = (bf16[1024,768]{1,0:T(8,128)(2,1)S(1)}, bf16[1024,768]{1,0:T(8,128)(2,1)S(1)}, u32[]{:S(2)}, u32[]{:S(2)}) collective-permute-start(bf16[1024,768]{1,0:T(8,128)(2,1)S(1)} %get-tuple-element.63), channel_id=1, source_target_pairs={{0,2},{1,3},{2,0},{3,1},{4,6},{5,7},{6,4},{7,5},{8,10},{9,11},{10,... | collective-permute-start | bytes 4718600 | tf_op jit(solution)/shard_map/ppermute | solution.py:198
  128.3 37.4 %collective-permute-start.5 = (bf16[1024,768]{1,0:T(8,128)(2,1)S(1)}, bf16[1024,768]{1,0:T(8,128)(2,1)S(1)}, u32[]{:S(2)}, u32[]{:S(2)}) collective-permute-start(bf16[1024,768]{1,0:T(8,128)(2,1)S(1)} %get-tuple-element.64), channel_id=1, source_target_pairs={{0,6},{1,7},{2,4},{3,5},{4,2},{5,3},{6,0},{7,1},{8,14},{9,15},{10,... | collective-permute-start | bytes 4718600 | tf_op jit(solution)/shard_map/ppermute | solution.py:198
  130.5 15.9 %collective-permute-start.6 = (bf16[256,512]{1,0:T(8,128)(2,1)S(1)}, bf16[256,512]{1,0:T(8,128)(2,1)S(1)}, u32[]{:S(2)}, u32[]{:S(2)}) collective-permute-start(bf16[256,512]{1,0:T(8,128)(2,1)S(1)} %copy-done.24), channel_id=1, source_target_pairs={{0,1},{1,0},{2,3},{3,2},{4,5},{5,4},{6,7},{7,6},{8,9},{9,8},{10,11... | collective-permute-start | bytes 786440 | tf_op jit(solution)/shard_map/ppermute | solution.py:198
  133.2 22.8 %collective-permute-start.7 = (bf16[256,512]{1,0:T(8,128)(2,1)S(1)}, bf16[256,512]{1,0:T(8,128)(2,1)S(1)}, u32[]{:S(2)}, u32[]{:S(2)}) collective-permute-start(bf16[256,512]{1,0:T(8,128)(2,1)S(1)} %get-tuple-element.68), channel_id=1, source_target_pairs={{0,1},{1,0},{2,3},{3,2},{4,5},{5,4},{6,7},{7,6},{8,9},{9,8},{10,11... | collective-permute-start | bytes 786440 | tf_op jit(solution)/shard_map/ppermute | solution.py:198
  163.8 6.5 %copy-start.6 = (bf16[1024,768]{1,0:T(8,128)(2,1)}, bf16[1024,768]{1,0:T(8,128)(2,1)S(1)}, u32[]{:S(2)}) copy-start(bf16[1024,768]{1,0:T(8,128)(2,1)S(1)} %collective-permute-done.4.refs_1_) | copy-start | bytes 4718596
  165.7 4.6 %copy-start.8 = (bf16[1024,768]{1,0:T(8,128)(2,1)}, bf16[1024,768]{1,0:T(8,128)(2,1)S(1)}, u32[]{:S(2)}) copy-start(bf16[1024,768]{1,0:T(8,128)(2,1)S(1)} %collective-permute-done.5.refs_2_) | copy-start | bytes 4718596
  170.3 0.8 copy-start.13
  171.1 22.0 %collective-permute-start.11 = (bf16[512,768]{1,0:T(8,128)(2,1)}, bf16[512,768]{1,0:T(8,128)(2,1)}, u32[]{:S(2)}, u32[]{:S(2)}) collective-permute-start(bf16[512,768]{1,0:T(8,128)(2,1)} %get-tuple-element.76), channel_id=1, source_target_pairs={{0,6},{1,7},{2,4},{3,5},{4,2},{5,3},{6,0},{7,1},{8,14},{9,15},{10,... | collective-permute-start | bytes 2359304 | tf_op jit(solution)/shard_map/ppermute | solution.py:198
  173.3 20.8 %collective-permute-start.12 = (bf16[512,768]{1,0:T(8,128)(2,1)}, bf16[512,768]{1,0:T(8,128)(2,1)}, u32[]{:S(2)}, u32[]{:S(2)}) collective-permute-start(bf16[512,768]{1,0:T(8,128)(2,1)} %get-tuple-element.77), channel_id=1, source_target_pairs={{0,2},{1,3},{2,0},{3,1},{4,6},{5,7},{6,4},{7,5},{8,10},{9,11},{10,... | collective-permute-start | bytes 2359304 | tf_op jit(solution)/shard_map/ppermute | solution.py:198
  173.3 20.8 %copy-start.7 = (bf16[1024,768]{1,0:T(8,128)(2,1)S(1)}, bf16[1024,768]{1,0:T(8,128)(2,1)}, u32[]{:S(2)}) copy-start(bf16[1024,768]{1,0:T(8,128)(2,1)} %copy-done.6) | copy-start | bytes 4718596
  173.3 20.8 %copy-start.9 = (bf16[1024,768]{1,0:T(8,128)(2,1)S(1)}, bf16[1024,768]{1,0:T(8,128)(2,1)}, u32[]{:S(2)}) copy-start(bf16[1024,768]{1,0:T(8,128)(2,1)} %copy-done.8) | copy-start | bytes 4718596
  177.2 37.0 %collective-permute-start.8 = (bf16[1024,384]{1,0:T(8,128)(2,1)S(1)}, bf16[1024,384]{1,0:T(8,128)(2,1)S(1)}, u32[]{:S(2)}, u32[]{:S(2)}) collective-permute-start(bf16[1024,384]{1,0:T(8,128)(2,1)S(1)} %get-tuple-element.73), channel_id=1, source_target_pairs={{0,2},{1,3},{2,0},{3,1},{4,6},{5,7},{6,4},{7,5},{8,10},{9,11},{10,... | collective-permute-start | bytes 2359304 | tf_op jit(solution)/shard_map/ppermute | solution.py:198
  179.3 34.9 %collective-permute-start.9 = (bf16[1024,384]{1,0:T(8,128)(2,1)S(1)}, bf16[1024,384]{1,0:T(8,128)(2,1)S(1)}, u32[]{:S(2)}, u32[]{:S(2)}) collective-permute-start(bf16[1024,384]{1,0:T(8,128)(2,1)S(1)} %get-tuple-element.74), channel_id=1, source_target_pairs={{0,6},{1,7},{2,4},{3,5},{4,2},{5,3},{6,0},{7,1},{8,14},{9,15},{10,... | collective-permute-start | bytes 2359304 | tf_op jit(solution)/shard_map/ppermute | solution.py:198
  180.4 33.8 %collective-permute-start.10 = (bf16[1024,256]{1,0:T(8,128)(2,1)S(1)}, bf16[1024,256]{1,0:T(8,128)(2,1)S(1)}, u32[]{:S(2)}, u32[]{:S(2)}) collective-permute-start(bf16[1024,256]{1,0:T(8,128)(2,1)S(1)} %get-tuple-element.75), channel_id=1, source_target_pairs={{0,1},{1,0},{2,3},{3,2},{4,5},{5,4},{6,7},{7,6},{8,9},{9,8},{10,11... | collective-permute-start | bytes 1572872 | tf_op jit(solution)/shard_map/ppermute | solution.py:198
  197.7 12.3 %collective-permute-start.13 = (bf16[256,768]{1,0:T(8,128)(2,1)S(1)}, bf16[256,768]{1,0:T(8,128)(2,1)S(1)}, u32[]{:S(2)}, u32[]{:S(2)}) collective-permute-start(bf16[256,768]{1,0:T(8,128)(2,1)S(1)} %get-tuple-element.81), channel_id=1, source_target_pairs={{0,1},{1,0},{2,3},{3,2},{4,5},{5,4},{6,7},{7,6},{8,9},{9,8},{10,11... | collective-permute-start | bytes 1179656 | tf_op jit(solution)/shard_map/ppermute | solution.py:198
  200.5 13.7 %collective-permute-start.14 = (bf16[256,768]{1,0:T(8,128)(2,1)S(1)}, bf16[256,768]{1,0:T(8,128)(2,1)S(1)}, u32[]{:S(2)}, u32[]{:S(2)}) collective-permute-start(bf16[256,768]{1,0:T(8,128)(2,1)S(1)} %get-tuple-element.82), channel_id=1, source_target_pairs={{0,1},{1,0},{2,3},{3,2},{4,5},{5,4},{6,7},{7,6},{8,9},{9,8},{10,11... | collective-permute-start | bytes 1179656 | tf_op jit(solution)/shard_map/ppermute | solution.py:198
  217.1 11.2 %collective-permute-start.15 = (bf16[512,384]{1,0:T(8,128)(2,1)S(1)}, bf16[512,384]{1,0:T(8,128)(2,1)S(1)}, u32[]{:S(2)}, u32[]{:S(2)}) collective-permute-start(bf16[512,384]{1,0:T(8,128)(2,1)S(1)} %get-tuple-element.85), channel_id=1, source_target_pairs={{0,6},{1,7},{2,4},{3,5},{4,2},{5,3},{6,0},{7,1},{8,14},{9,15},{10,... | collective-permute-start | bytes 1179656 | tf_op jit(solution)/shard_map/ppermute | solution.py:198
  219.2 9.3 %collective-permute-start.16 = (bf16[512,384]{1,0:T(8,128)(2,1)S(1)}, bf16[512,384]{1,0:T(8,128)(2,1)S(1)}, u32[]{:S(2)}, u32[]{:S(2)}) collective-permute-start(bf16[512,384]{1,0:T(8,128)(2,1)S(1)} %get-tuple-element.86), channel_id=1, source_target_pairs={{0,1},{1,0},{2,3},{3,2},{4,5},{5,4},{6,7},{7,6},{8,9},{9,8},{10,11... | collective-permute-start | bytes 1179656 | tf_op jit(solution)/shard_map/ppermute | solution.py:198
  222.0 6.4 %collective-permute-start.17 = (bf16[512,256]{1,0:T(8,128)(2,1)S(1)}, bf16[512,256]{1,0:T(8,128)(2,1)S(1)}, u32[]{:S(2)}, u32[]{:S(2)}) collective-permute-start(bf16[512,256]{1,0:T(8,128)(2,1)S(1)} %get-tuple-element.87), channel_id=1, source_target_pairs={{0,2},{1,3},{2,0},{3,1},{4,6},{5,7},{6,4},{7,5},{8,10},{9,11},{10,... | collective-permute-start | bytes 786440 | tf_op jit(solution)/shard_map/ppermute | solution.py:198
  231.3 9.0 %collective-permute-start.18 = (bf16[256,384]{1,0:T(8,128)(2,1)S(1)}, bf16[256,384]{1,0:T(8,128)(2,1)S(1)}, u32[]{:S(2)}, u32[]{:S(2)}) collective-permute-start(bf16[256,384]{1,0:T(8,128)(2,1)S(1)} %get-tuple-element.92), channel_id=1, source_target_pairs={{0,1},{1,0},{2,3},{3,2},{4,5},{5,4},{6,7},{7,6},{8,9},{9,8},{10,11... | collective-permute-start | bytes 589832 | tf_op jit(solution)/shard_map/ppermute | solution.py:198
  234.1 6.2 %collective-permute-start.19 = (bf16[256,384]{1,0:T(8,128)(2,1)S(1)}, bf16[256,384]{1,0:T(8,128)(2,1)S(1)}, u32[]{:S(2)}, u32[]{:S(2)}) collective-permute-start(bf16[256,384]{1,0:T(8,128)(2,1)S(1)} %get-tuple-element.93), channel_id=1, source_target_pairs={{0,2},{1,3},{2,0},{3,1},{4,6},{5,7},{6,4},{7,5},{8,10},{9,11},{10,... | collective-permute-start | bytes 589832 | tf_op jit(solution)/shard_map/ppermute | solution.py:198
  234.1 6.2 %collective-permute-start.20 = (bf16[256,256]{1,0:T(8,128)(2,1)S(1)}, bf16[256,256]{1,0:T(8,128)(2,1)S(1)}, u32[]{:S(2)}, u32[]{:S(2)}) collective-permute-start(bf16[256,256]{1,0:T(8,128)(2,1)S(1)} %get-tuple-element.94), channel_id=1, source_target_pairs={{0,6},{1,7},{2,4},{3,5},{4,2},{5,3},{6,0},{7,1},{8,14},{9,15},{10,... | collective-permute-start | bytes 393224 | tf_op jit(solution)/shard_map/ppermute | solution.py:198
  240.3 1.0 copy-start.14
  (1 other events, 0.7 us)

commit v4 on v3

--- a/solution.py
+++ b/solution.py
@@ -10,7 +10,7 @@
 EXP_DEV = 4
 TWO = ((0, 1, 2), (1, 0, 2))
 THREE = ((0, 1, 2), (1, 2, 0), (2, 0, 1))
-WIDTHS = ((512, 512), (768, 768), (384, 384, 256))
+WIDTHS = ((384, 384), (768, 768), (512, 512, 256))
 ORDERS = (TWO, TWO, THREE)
 VMEM = 16 * 1024 * 1024
 STEPS = (
@@ -72,13 +72,23 @@
     )
 
 
-def terms(kind, orders, size, place_ref, hidden_ref, ins, outs):
+def terms(kind, orders, size, place_ref, hidden_ref, ins, outs, sems):
     arrived_ref, came = ins[0], ins[1:]
-    start = 0
+    starts = [sum(out.shape[1] for out in outs[:part]) for part in range(len(orders))]
+    spans = [pl.ds(start, out.shape[1]) for start, out in zip(starts, outs)]
+    if kind == 1:
+        held_ref = outs[-1]
+        copies = [
+            pltpu.make_async_copy(arrived_ref.at[:, span], held_ref.at[:, span], sems.at[part])
+            for part, span in enumerate(spans)
+        ]
+        for copy in copies:
+            copy.start()
+        arrived_ref = held_ref
     for part, order in enumerate(orders):
-        width = outs[part].shape[1]
-        rows = arrived_ref[:, start : start + width]
-        start += width
+        if kind == 1:
+            copies[part].wait()
+        rows = arrived_ref[:, spans[part]]
         earlier = [came[e * len(orders) + part] for e in range(kind - 1)]
         if kind == 1:
             targets = [(outs[part], (1, i, j)) for i in (1, 0) for j in (1, 0)]
@@ -100,9 +110,12 @@
             filled[id(out_ref)] = at + size
 
 
-def last_sum(ins, outs):
+def last_sum(parts, ins, outs):
     start = 0
-    parts = len(ins) // 2
+    for done in ins[2 * parts :]:
+        width = done.shape[1]
+        outs[0][:, start : start + width] = done[...]
+        start += width
     for part in range(parts):
         width = ins[part].shape[1]
         total = ins[part][...] + ins[parts + part][...].astype(jnp.float32)
@@ -116,9 +129,10 @@
     i = o = 0
     for kind, orders, n_in, n_out in jobs:
         if kind == 4:
-            last_sum(ins[i : i + n_in], outs[o : o + n_out])
+            last_sum(len(orders), ins[i : i + n_in], outs[o : o + n_out])
         else:
-            terms(kind, orders, size, place_ref, hidden_ref, ins[i : i + n_in], outs[o : o + n_out])
+            given, made = ins[i : i + n_in], outs[o : o + n_out]
+            terms(kind, orders, size, place_ref, hidden_ref, given, made, refs[-1])
         i, o = i + n_in, o + n_out
 
 
@@ -129,17 +143,20 @@
     vmem, anywhere = pl.BlockSpec(memory_space=pltpu.VMEM), pl.BlockSpec(memory_space=pl.ANY)
     res = pl.pallas_call(
         functools.partial(step_kernel, size, counts),
-        in_specs=[pl.BlockSpec(memory_space=pltpu.SMEM), vmem] + [vmem] * len(ins) + [anywhere],
+        in_specs=[pl.BlockSpec(memory_space=pltpu.SMEM), vmem]
+        + [anywhere if kind == 1 else vmem for kind, _, given, _ in jobs for _ in given]
+        + [anywhere],
         out_specs=[vmem] * len(shapes) + [anywhere],
         out_shape=shapes + [jax.ShapeDtypeStruct(token.shape, token.dtype)],
         input_output_aliases={2 + len(ins): len(shapes)},
+        scratch_shapes=[pltpu.SemaphoreType.DMA((3,))],
         compiler_params=pltpu.CompilerParams(vmem_limit_bytes=VMEM),
     )(place, hidden, *ins, token)
     made, at = [], 0
     for _, _, _, n_out in counts:
         made.append(res[at : at + n_out])
         at += n_out
-    return made, res[-1]
+    return made, res[len(shapes)]
 
 
 def shards(grad_out, route_probs, routes, hidden_saved):
@@ -183,9 +200,14 @@
         jobs = []
         for kind, c in names:
             if kind == 4:
-                jobs.append((4, ORDERS[c], keep[c] + came[c][2 * len(ORDERS[c]) :], [shape(size, sum(WIDTHS[c]))]))
+                given, width = keep[c] + came[c][2 * len(ORDERS[c]) :], sum(WIDTHS[c])
+                if c == len(WIDTHS) - 1:
+                    given, width = given + [out[i] for i in range(c)], model_cols
+                jobs.append((4, ORDERS[c], given, [shape(size, width)]))
                 continue
             made = [shape(hidden >> kind, w) for w in WIDTHS[c]]
+            if kind == 1:
+                made.append(shape(slot_count, sum(WIDTHS[c])))
             if kind == 3:
                 made += [shape(size, w, jnp.float32) for w in WIDTHS[c]]
             jobs.append((kind, ORDERS[c], [arrived[c]] + came[c], made))
@@ -197,8 +219,10 @@
             came[c] = came[c] + [
                 lax.ppermute(m, "dp", partners[order[kind - 1]]) for m, order in zip(made, ORDERS[c])
             ]
+            if kind == 1:
+                arrived[c] = made[-1]
             keep[c] = list(made[len(ORDERS[c]) :])
-    return jnp.concatenate([out[c] for c in range(len(WIDTHS))], axis=1)
+    return out[len(WIDTHS) - 1]
 
 
 def solution(mesh):

time: 243 us -> 235 us (0.967)
  waiting for transfers between devices: 142 us -> 136 us
    ppermute x21, waiting for transfers between devices: 103 us -> 97 us  [shards(): lax.ppermute(m, 'dp', partners[order[kind - 1]])]
    unnamed x50 -> x54, local copies, waits for them, and re-layouts: 12.6 us -> 13.1 us
  transfers between devices with their start and end apart: 24 -> 24, of which waited for: 17 -> 19; matrix products, arithmetic and copies ran while one was open for 0% -> 0% of each run, Pallas kernels for 10% -> 10%
where the time goes in v4:
time: 235 us
  waiting for transfers between devices  136 us (58%)
  starting transfers between devices  55.7 us (24%)
  Pallas kernels  29.9 us (13%)
  local copies, waits for them, and re-layouts  13.1 us (6%)
    ppermute x21, waiting for transfers between devices, shards(): lax.ppermute(m, 'dp', partners[order[kind - 1]])  97 us
    all_to_all x3, waiting for transfers between devices, shards(): rows = lax.all_to_all(rows, 'ep', split_axis=0, concat_axis=0, tiled=True)  38.7 us
    ppermute x21, starting transfers between devices, shards(): lax.ppermute(m, 'dp', partners[order[kind - 1]])  34.3 us
    pallas_call x10, Pallas kernels, step(): pl.pallas_call(functools.partial(step_kernel, size, counts), in_specs=[pl...  27.4 us
    all_to_all x3, starting transfers between devices, shards(): rows = lax.all_to_all(rows, 'ep', split_axis=0, concat_axis=0, tiled=True)  21.4 us
    unnamed x54, local copies, waits for them, and re-layouts  13.1 us
  transfers between devices with their start and end apart: 24, of which 19 were waited for; matrix products, arithmetic and copies ran while one was open for 0% of the time, Pallas kernels for 10%

profile of v4, /device:TPU:32, one launch (start us, length us, event | category | flops | bytes accessed | tf_op | source)
XLA Modules:
  0.0 234.9 jit_solution(14216686283851762652)
XLA Ops:
  0.0 1.3 copy-done.1
  4.4 9.7 %all-to-all-start = ((bf16[32,24,768]{2,1,0:T(8,128)(2,1)}), bf16[32,24,768]{2,1,0:T(8,128)(2,1)S(1)}, u32[]{:S(2)}, u32[]{:S(2)}) async-start(bf16[32,24,768]{2,1,0:T(8,128)(2,1)} %bitcast.24), calls=%async_computation | async-start | bytes 2359296 | tf_op jit(solution)/shard_map/all_to_all | solution.py:197
  15.1 1.4 copy-done.12
  16.5 28.4 %all-to-all-done = bf16[32,24,768]{2,1,0:T(8,128)(2,1)S(1)} async-done(((bf16[32,24,768]{2,1,0:T(8,128)(2,1)}), bf16[32,24,768]{2,1,0:T(8,128)(2,1)S(1)}, u32[]{:S(2)}, u32[]{:S(2)}) %all-to-all-start) | async-done | bytes 1179680 | tf_op jit(solution)/shard_map/all_to_all | solution.py:197
  46.0 5.9 %all-to-all-start.2 = ((bf16[32,24,1536]{2,1,0:T(8,128)(2,1)}), bf16[32,24,1536]{2,1,0:T(8,128)(2,1)}, u32[]{:S(2)}, u32[]{:S(2)}) async-start(bf16[32,24,1536]{2,1,0:T(8,128)(2,1)} %bitcast.22), calls=%async_computation.2 | async-start | bytes 4718592 | tf_op jit(solution)/shard_map/all_to_all | solution.py:197
  52.0 1.3 copy-done.11
  53.3 2.8 %shard_map.48 = (bf16[1024,384]{1,0:T(8,128)(2,1)S(1)}, bf16[1024,384]{1,0:T(8,128)(2,1)S(1)}, bf16[768,768]{1,0:T(8,128)(2,1)S(1)}, s32[8,128]{1,0:T(8,128)S(1)}) custom-call(s32[2]{0:T(128)S(1)} %pad_add_fusion.place_ref, bf16[768,2048]{1,0:T(8,128)(2,1)S(1)} %bitcast.11, bf16[768,768]{1,0:T(8,128)(2,1)S(1)} %bitcast.21, ...), custom_call_target="tpu_custom_call", output_to_operand_aliasing={{3}: (3, {})} | custom-call | tf_op jit(solution)/shard_map/pallas_call | solution.py:144
  56.1 1.7 collective-permute-start
  57.7 2.2 collective-permute-start.1
  59.9 15.8 %collective-permute-done.refs_1_ = bf16[1024,384]{1,0:T(8,128)(2,1)S(1)} collective-permute-done((bf16[1024,384]{1,0:T(8,128)(2,1)S(1)}, bf16[1024,384]{1,0:T(8,128)(2,1)S(1)}, u32[]{:S(2)}, u32[]{:S(2)}) %collective-permute-start) | collective-permute-done | bytes 786464 | tf_op jit(solution)/shard_map/ppermute | solution.py:220
  75.7 2.5 %collective-permute-done.1.refs_2_ = bf16[1024,384]{1,0:T(8,128)(2,1)S(1)} collective-permute-done((bf16[1024,384]{1,0:T(8,128)(2,1)S(1)}, bf16[1024,384]{1,0:T(8,128)(2,1)S(1)}, u32[]{:S(2)}, u32[]{:S(2)}) %collective-permute-start.1) | collective-permute-done | bytes 786464 | tf_op jit(solution)/shard_map/ppermute | solution.py:220
  78.2 1.6 shard_map.49
  79.9 2.2 collective-permute-start.2
  82.1 9.2 %collective-permute-done.2.refs_3_ = bf16[512,384]{1,0:T(8,128)(2,1)S(1)} collective-permute-done((bf16[512,384]{1,0:T(8,128)(2,1)S(1)}, bf16[512,384]{1,0:T(8,128)(2,1)S(1)}, u32[]{:S(2)}, u32[]{:S(2)}) %collective-permute-start.2) | collective-permute-done | bytes 393248 | tf_op jit(solution)/shard_map/ppermute | solution.py:220
  92.0 1.6 shard_map.50
  96.6 1.3 copy-done.13
  97.9 10.3 %all-to-all-done.2 = bf16[32,24,1536]{2,1,0:T(8,128)(2,1)} async-done(((bf16[32,24,1536]{2,1,0:T(8,128)(2,1)}), bf16[32,24,1536]{2,1,0:T(8,128)(2,1)}, u32[]{:S(2)}, u32[]{:S(2)}) %all-to-all-start.2) | async-done | bytes 2359328 | tf_op jit(solution)/shard_map/all_to_all | solution.py:197
  108.2 5.8 %all-to-all-start.1 = ((bf16[32,24,1280]{2,1,0:T(8,128)(2,1)}), bf16[32,24,1280]{2,1,0:T(8,128)(2,1)}, u32[]{:S(2)}, u32[]{:S(2)}) async-start(bf16[32,24,1280]{2,1,0:T(8,128)(2,1)} %bitcast.23), calls=%async_computation.1 | async-start | bytes 3932160 | tf_op jit(solution)/shard_map/all_to_all | solution.py:197
  114.0 4.7 %shard_map.52 = (bf16[1024,768]{1,0:T(8,128)(2,1)S(1)}, bf16[1024,768]{1,0:T(8,128)(2,1)S(1)}, bf16[768,1536]{1,0:T(8,128)(2,1)S(1)}, s32[8,128]{1,0:T(8,128)S(1)}) custom-call(s32[2]{0:T(128)S(1)} %pad_add_fusion.place_ref, bf16[768,2048]{1,0:T(8,128)(2,1)S(1)} %bitcast.14, bf16[768,1536]{1,0:T(8,128)(2,1)} %bitcast.10.refs_0_, ...), custom_call_target="tpu_custom_call", output_to_operand_aliasing={{3}: (3, {})} | custom-call | tf_op jit(solution)/shard_map/pallas_call | solution.py:144
  118.8 1.7 collective-permute-start.4
  120.4 2.2 collective-permute-start.5
  122.6 2.7 %collective-permute-start.6 = (bf16[256,384]{1,0:T(8,128)(2,1)S(1)}, bf16[256,384]{1,0:T(8,128)(2,1)S(1)}, u32[]{:S(2)}, u32[]{:S(2)}) collective-permute-start(bf16[256,384]{1,0:T(8,128)(2,1)S(1)} %copy-done.26), channel_id=1, source_target_pairs={{0,1},{1,0},{2,3},{3,2},{4,5},{5,4},{6,7},{7,6},{8,9},{9,8},{10,11... | collective-permute-start | bytes 589832 | tf_op jit(solution)/shard_map/ppermute | solution.py:220
  126.1 11.8 %collective-permute-done.6.refs_5_ = bf16[256,384]{1,0:T(8,128)(2,1)S(1)} collective-permute-done((bf16[256,384]{1,0:T(8,128)(2,1)S(1)}, bf16[256,384]{1,0:T(8,128)(2,1)S(1)}, u32[]{:S(2)}, u32[]{:S(2)}) %collective-permute-start.6) | collective-permute-done | bytes 196640 | tf_op jit(solution)/shard_map/ppermute | solution.py:220
  137.9 4.1 %collective-permute-done.7.refs_6_ = bf16[256,384]{1,0:T(8,128)(2,1)S(1)} collective-permute-done((bf16[256,384]{1,0:T(8,128)(2,1)S(1)}, bf16[256,384]{1,0:T(8,128)(2,1)S(1)}, u32[]{:S(2)}, u32[]{:S(2)}) %collective-permute-start.7) | collective-permute-done | bytes 196640 | tf_op jit(solution)/shard_map/ppermute | solution.py:220
  142.0 13.3 %collective-permute-done.4.refs_1_ = bf16[1024,768]{1,0:T(8,128)(2,1)S(1)} collective-permute-done((bf16[1024,768]{1,0:T(8,128)(2,1)S(1)}, bf16[1024,768]{1,0:T(8,128)(2,1)S(1)}, u32[]{:S(2)}, u32[]{:S(2)}) %collective-permute-start.4) | collective-permute-done | bytes 1572896 | tf_op jit(solution)/shard_map/ppermute | solution.py:220
  155.3 2.5 %collective-permute-done.5.refs_2_ = bf16[1024,768]{1,0:T(8,128)(2,1)S(1)} collective-permute-done((bf16[1024,768]{1,0:T(8,128)(2,1)S(1)}, bf16[1024,768]{1,0:T(8,128)(2,1)S(1)}, u32[]{:S(2)}, u32[]{:S(2)}) %collective-permute-start.5) | collective-permute-done | bytes 1572896 | tf_op jit(solution)/shard_map/ppermute | solution.py:220
  157.8 2.9 %shard_map.53 = (bf16[512,768]{1,0:T(8,128)(2,1)}, bf16[512,768]{1,0:T(8,128)(2,1)}, bf16[256,768]{1,0:T(8,128)(2,1)S(1)}, s32[8,128]{1,0:T(8,128)S(1)}) custom-call(s32[2]{0:T(128)S(1)} %pad_add_fusion.place_ref, bf16[768,2048]{1,0:T(8,128)(2,1)S(1)} %bitcast.15, bf16[768,1536]{1,0:T(8,128)(2,1)S(1)} %get-tuple-element.68.refs_0_, ...), custom_call_target="tpu_custom_call", output_to_operand_aliasing={{3}: (9, {})} | custom-call | tf_op jit(solution)/shard_map/pallas_call | solution.py:144
  161.6 2.2 collective-permute-start.11
  163.8 4.7 %shard_map.54 = (bf16[1024,512]{1,0:T(8,128)(2,1)S(1)}, bf16[1024,512]{1,0:T(8,128)(2,1)S(1)}, bf16[1024,256]{1,0:T(8,128)(2,1)S(1)}, bf16[768,1280]{1,0:T(8,128)(2,1)S(1)}, s32[8,128]{1,0:T(8,128)S(1)}) custom-call(s32[2]{0:T(128)S(1)} %pad_add_fusion.place_ref, bf16[768,2048]{1,0:T(8,128)(2,1)S(1)} %bitcast.16, ...), custom_call_target="tpu_custom_call", output_to_operand_aliasing={{4}: (3, {})} | custom-call | tf_op jit(solution)/shard_map/pallas_call | solution.py:144
  168.5 2.1 collective-permute-start.8
  170.6 1.1 collective-permute-start.9
  171.6 2.7 %collective-permute-start.10 = (bf16[1024,256]{1,0:T(8,128)(2,1)S(1)}, bf16[1024,256]{1,0:T(8,128)(2,1)S(1)}, u32[]{:S(2)}, u32[]{:S(2)}) collective-permute-start(bf16[1024,256]{1,0:T(8,128)(2,1)S(1)} %get-tuple-element.80), channel_id=1, source_target_pairs={{0,1},{1,0},{2,3},{3,2},{4,5},{5,4},{6,7},{7,6},{8,9},{9,8},{10,11... | collective-permute-start | bytes 1572872 | tf_op jit(solution)/shard_map/ppermute | solution.py:220
  174.4 9.2 %collective-permute-done.11.refs_3_ = bf16[512,768]{1,0:T(8,128)(2,1)} collective-permute-done((bf16[512,768]{1,0:T(8,128)(2,1)}, bf16[512,768]{1,0:T(8,128)(2,1)}, u32[]{:S(2)}, u32[]{:S(2)}) %collective-permute-start.11) | collective-permute-done | bytes 786464 | tf_op jit(solution)/shard_map/ppermute | solution.py:220
  184.5 1.4 copy-done.9
  185.9 2.9 %shard_map.55 = (bf16[256,768]{1,0:T(8,128)(2,1)S(1)}, bf16[256,768]{1,0:T(8,128)(2,1)S(1)}, f32[256,768]{1,0:T(8,128)S(1)}, f32[256,768]{1,0:T(8,128)S(1)}, s32[8,128]{1,0:T(8,128)S(1)}) custom-call(s32[2]{0:T(128)S(1)} %pad_add_fusion.place_ref, bf16[768,2048]{1,0:T(8,128)(2,1)S(1)} %bitcast.17, ...), custom_call_target="tpu_custom_call", output_to_operand_aliasing={{4}: (7, {})} | custom-call | tf_op jit(solution)/shard_map/pallas_call | solution.py:144
  188.9 3.0 %collective-permute-start.13 = (bf16[256,768]{1,0:T(8,128)(2,1)S(1)}, bf16[256,768]{1,0:T(8,128)(2,1)S(1)}, u32[]{:S(2)}, u32[]{:S(2)}) collective-permute-start(bf16[256,768]{1,0:T(8,128)(2,1)S(1)} %get-tuple-element.86), channel_id=1, source_target_pairs={{0,1},{1,0},{2,3},{3,2},{4,5},{5,4},{6,7},{7,6},{8,9},{9,8},{10,11... | collective-permute-start | bytes 1179656 | tf_op jit(solution)/shard_map/ppermute | solution.py:220
  192.7 8.9 %collective-permute-done.13.refs_6_ = bf16[256,768]{1,0:T(8,128)(2,1)S(1)} collective-permute-done((bf16[256,768]{1,0:T(8,128)(2,1)S(1)}, bf16[256,768]{1,0:T(8,128)(2,1)S(1)}, u32[]{:S(2)}, u32[]{:S(2)}) %collective-permute-start.13) | collective-permute-done | bytes 393248 | tf_op jit(solution)/shard_map/ppermute | solution.py:220
  201.6 4.2 %collective-permute-done.14.refs_7_ = bf16[256,768]{1,0:T(8,128)(2,1)S(1)} collective-permute-done((bf16[256,768]{1,0:T(8,128)(2,1)S(1)}, bf16[256,768]{1,0:T(8,128)(2,1)S(1)}, u32[]{:S(2)}, u32[]{:S(2)}) %collective-permute-start.14) | collective-permute-done | bytes 393248 | tf_op jit(solution)/shard_map/ppermute | solution.py:220
  205.8 2.1 shard_map.56
  207.9 1.9 collective-permute-start.15
  209.8 2.7 %collective-permute-start.16 = (bf16[512,512]{1,0:T(8,128)(2,1)S(1)}, bf16[512,512]{1,0:T(8,128)(2,1)S(1)}, u32[]{:S(2)}, u32[]{:S(2)}) collective-permute-start(bf16[512,512]{1,0:T(8,128)(2,1)S(1)} %get-tuple-element.90), channel_id=1, source_target_pairs={{0,1},{1,0},{2,3},{3,2},{4,5},{5,4},{6,7},{7,6},{8,9},{9,8},{10,11... | collective-permute-start | bytes 1572872 | tf_op jit(solution)/shard_map/ppermute | solution.py:220
  212.5 6.4 %collective-permute-done.17.refs_6_ = bf16[512,256]{1,0:T(8,128)(2,1)S(1)} collective-permute-done((bf16[512,256]{1,0:T(8,128)(2,1)S(1)}, bf16[512,256]{1,0:T(8,128)(2,1)S(1)}, u32[]{:S(2)}, u32[]{:S(2)}) %collective-permute-start.17) | collective-permute-done | bytes 262176 | tf_op jit(solution)/shard_map/ppermute | solution.py:220
  219.8 1.8 collective-permute-done.16.refs_5_
  221.6 1.9 shard_map.57
  223.5 2.9 %collective-permute-start.18 = (bf16[256,512]{1,0:T(8,128)(2,1)S(1)}, bf16[256,512]{1,0:T(8,128)(2,1)S(1)}, u32[]{:S(2)}, u32[]{:S(2)}) collective-permute-start(bf16[256,512]{1,0:T(8,128)(2,1)S(1)} %get-tuple-element.96), channel_id=1, source_target_pairs={{0,1},{1,0},{2,3},{3,2},{4,5},{5,4},{6,7},{7,6},{8,9},{9,8},{10,11... | collective-permute-start | bytes 786440 | tf_op jit(solution)/shard_map/ppermute | solution.py:220
  226.4 1.5 collective-permute-start.20
  227.9 4.7 %collective-permute-done.20.refs_5_ = bf16[256,256]{1,0:T(8,128)(2,1)S(1)} collective-permute-done((bf16[256,256]{1,0:T(8,128)(2,1)S(1)}, bf16[256,256]{1,0:T(8,128)(2,1)S(1)}, u32[]{:S(2)}, u32[]{:S(2)}) %collective-permute-start.20) | collective-permute-done | bytes 131104 | tf_op jit(solution)/shard_map/ppermute | solution.py:220
  232.8 2.0 shard_map.58
  (69 shorter events, 13.3 us)
Async XLA Ops:
  0.0 1.3 copy-start.1
  1.3 0.7 copy-start.19
  2.7 11.3 %copy-start.2 = (bf16[192,3584]{1,0:T(8,128)(2,1)S(1)}, bf16[192,3584]{1,0:T(8,128)(2,1)}, u32[]{:S(2)}) copy-start(bf16[192,3584]{1,0:T(8,128)(2,1)} %grad_ref.5) | copy-start | bytes 4128772
  3.4 1.0 copy-start.14
  4.4 40.5 %all-to-all-start = ((bf16[32,24,768]{2,1,0:T(8,128)(2,1)}), bf16[32,24,768]{2,1,0:T(8,128)(2,1)S(1)}, u32[]{:S(2)}, u32[]{:S(2)}) async-start(bf16[32,24,768]{2,1,0:T(8,128)(2,1)} %bitcast.24), calls=%async_computation | async-start | bytes 2359296 | tf_op jit(solution)/shard_map/all_to_all | solution.py:197
  15.0 1.5 copy-start.12
  44.9 1.0 copy-start.10
  46.0 6.0 %copy-start = (bf16[1,768,2048]{2,1,0:T(8,128)(2,1)S(1)}, bf16[1,768,2048]{2,1,0:T(8,128)(2,1)}, u32[]{:S(2)}) copy-start(bf16[1,768,2048]{2,1,0:T(8,128)(2,1)} %param.7) | copy-start | bytes 9437188
  46.0 62.2 %all-to-all-start.2 = ((bf16[32,24,1536]{2,1,0:T(8,128)(2,1)}), bf16[32,24,1536]{2,1,0:T(8,128)(2,1)}, u32[]{:S(2)}, u32[]{:S(2)}) async-start(bf16[32,24,1536]{2,1,0:T(8,128)(2,1)} %bitcast.22), calls=%async_computation.2 | async-start | bytes 4718592 | tf_op jit(solution)/shard_map/all_to_all | solution.py:197
  52.0 1.3 copy-start.11
  56.1 19.7 %collective-permute-start = (bf16[1024,384]{1,0:T(8,128)(2,1)S(1)}, bf16[1024,384]{1,0:T(8,128)(2,1)S(1)}, u32[]{:S(2)}, u32[]{:S(2)}) collective-permute-start(bf16[1024,384]{1,0:T(8,128)(2,1)S(1)} %get-tuple-element.58), channel_id=1, source_target_pairs={{0,2},{1,3},{2,0},{3,1},{4,6},{5,7},{6,4},{7,5},{8,10},{9,11},{10,... | collective-permute-start | bytes 2359304 | tf_op jit(solution)/shard_map/ppermute | solution.py:220
  57.7 20.5 %collective-permute-start.1 = (bf16[1024,384]{1,0:T(8,128)(2,1)S(1)}, bf16[1024,384]{1,0:T(8,128)(2,1)S(1)}, u32[]{:S(2)}, u32[]{:S(2)}) collective-permute-start(bf16[1024,384]{1,0:T(8,128)(2,1)S(1)} %get-tuple-element.59), channel_id=1, source_target_pairs={{0,6},{1,7},{2,4},{3,5},{4,2},{5,3},{6,0},{7,1},{8,14},{9,15},{10,... | collective-permute-start | bytes 2359304 | tf_op jit(solution)/shard_map/ppermute | solution.py:220
  79.9 11.4 %collective-permute-start.2 = (bf16[512,384]{1,0:T(8,128)(2,1)S(1)}, bf16[512,384]{1,0:T(8,128)(2,1)S(1)}, u32[]{:S(2)}, u32[]{:S(2)}) collective-permute-start(bf16[512,384]{1,0:T(8,128)(2,1)S(1)} %get-tuple-element.61), channel_id=1, source_target_pairs={{0,6},{1,7},{2,4},{3,5},{4,2},{5,3},{6,0},{7,1},{8,14},{9,15},{10,... | collective-permute-start | bytes 1179656 | tf_op jit(solution)/shard_map/ppermute | solution.py:220
  82.1 9.8 %collective-permute-start.3 = (bf16[512,384]{1,0:T(8,128)(2,1)S(1)}, bf16[512,384]{1,0:T(8,128)(2,1)S(1)}, u32[]{:S(2)}, u32[]{:S(2)}) collective-permute-start(bf16[512,384]{1,0:T(8,128)(2,1)S(1)} %get-tuple-element.62), channel_id=1, source_target_pairs={{0,2},{1,3},{2,0},{3,1},{4,6},{5,7},{6,4},{7,5},{8,10},{9,11},{10,... | collective-permute-start | bytes 1179656 | tf_op jit(solution)/shard_map/ppermute | solution.py:220
  92.0 3.8 %copy-start.3 = (bf16[192,3584]{1,0:T(8,128)(2,1)S(1)}, bf16[192,3584]{1,0:T(8,128)(2,1)}, u32[]{:S(2)}) copy-start(bf16[192,3584]{1,0:T(8,128)(2,1)} %grad_ref.5) | copy-start | bytes 4128772
  92.0 3.8 %copy-start.20 = (s32[192,8]{0,1:T(8,128)S(1)}, s32[192,8]{0,1:T(8,128)}, u32[]{:S(2)}) copy-start(s32[192,8]{0,1:T(8,128)} %param.6) | copy-start | bytes 18436
  92.0 3.8 %copy-start.22 = (f32[192,8]{0,1:T(8,128)S(1)}, f32[192,8]{0,1:T(8,128)}, u32[]{:S(2)}) copy-start(f32[192,8]{0,1:T(8,128)} %param.5) | copy-start | bytes 18436
  93.6 0.8 copy-start.15
  96.6 1.3 copy-start.13
  108.2 55.6 %all-to-all-start.1 = ((bf16[32,24,1280]{2,1,0:T(8,128)(2,1)}), bf16[32,24,1280]{2,1,0:T(8,128)(2,1)}, u32[]{:S(2)}, u32[]{:S(2)}) async-start(bf16[32,24,1280]{2,1,0:T(8,128)(2,1)} %bitcast.23), calls=%async_computation.1 | async-start | bytes 3932160 | tf_op jit(solution)/shard_map/all_to_all | solution.py:197
  114.0 8.6 %copy-start.26 = (bf16[256,384]{1,0:T(8,128)(2,1)S(1)}, bf16[256,384]{1,0:T(8,128)(2,1)}, u32[]{:S(2)}) copy-start(bf16[256,384]{1,0:T(8,128)(2,1)} %copy-done.25) | copy-start | bytes 589828
  114.0 11.4 %copy-start.24 = (bf16[256,384]{1,0:T(8,128)(2,1)S(1)}, bf16[256,384]{1,0:T(8,128)(2,1)}, u32[]{:S(2)}) copy-start(bf16[256,384]{1,0:T(8,128)(2,1)} %copy-done.23) | copy-start | bytes 589828
  114.0 43.8 %copy-start.16 = (f32[256,384]{1,0:T(8,128)S(1)}, f32[256,384]{1,0:T(8,128)}, u32[]{:S(2)}) copy-start(f32[256,384]{1,0:T(8,128)} %copy-done.15) | copy-start | bytes 1179652
  118.8 42.0 %copy-start.4 = (bf16[768,1536]{1,0:T(8,128)(2,1)}, bf16[768,1536]{1,0:T(8,128)(2,1)S(1)}, u32[]{:S(2)}) copy-start(bf16[768,1536]{1,0:T(8,128)(2,1)S(1)} %get-tuple-element.68.refs_0_) | copy-start | bytes 7077892
  118.8 36.5 %collective-permute-start.4 = (bf16[1024,768]{1,0:T(8,128)(2,1)S(1)}, bf16[1024,768]{1,0:T(8,128)(2,1)S(1)}, u32[]{:S(2)}, u32[]{:S(2)}) collective-permute-start(bf16[1024,768]{1,0:T(8,128)(2,1)S(1)} %get-tuple-element.69), channel_id=1, source_target_pairs={{0,2},{1,3},{2,0},{3,1},{4,6},{5,7},{6,4},{7,5},{8,10},{9,11},{10,... | collective-permute-start | bytes 4718600 | tf_op jit(solution)/shard_map/ppermute | solution.py:220
  120.4 37.4 %collective-permute-start.5 = (bf16[1024,768]{1,0:T(8,128)(2,1)S(1)}, bf16[1024,768]{1,0:T(8,128)(2,1)S(1)}, u32[]{:S(2)}, u32[]{:S(2)}) collective-permute-start(bf16[1024,768]{1,0:T(8,128)(2,1)S(1)} %get-tuple-element.70), channel_id=1, source_target_pairs={{0,6},{1,7},{2,4},{3,5},{4,2},{5,3},{6,0},{7,1},{8,14},{9,15},{10,... | collective-permute-start | bytes 4718600 | tf_op jit(solution)/shard_map/ppermute | solution.py:220
  122.6 15.3 %collective-permute-start.6 = (bf16[256,384]{1,0:T(8,128)(2,1)S(1)}, bf16[256,384]{1,0:T(8,128)(2,1)S(1)}, u32[]{:S(2)}, u32[]{:S(2)}) collective-permute-start(bf16[256,384]{1,0:T(8,128)(2,1)S(1)} %copy-done.26), channel_id=1, source_target_pairs={{0,1},{1,0},{2,3},{3,2},{4,5},{5,4},{6,7},{7,6},{8,9},{9,8},{10,11... | collective-permute-start | bytes 589832 | tf_op jit(solution)/shard_map/ppermute | solution.py:220
  125.3 16.7 %collective-permute-start.7 = (bf16[256,384]{1,0:T(8,128)(2,1)S(1)}, bf16[256,384]{1,0:T(8,128)(2,1)S(1)}, u32[]{:S(2)}, u32[]{:S(2)}) collective-permute-start(bf16[256,384]{1,0:T(8,128)(2,1)S(1)} %copy-done.24), channel_id=1, source_target_pairs={{0,1},{1,0},{2,3},{3,2},{4,5},{5,4},{6,7},{7,6},{8,9},{9,8},{10,11... | collective-permute-start | bytes 589832 | tf_op jit(solution)/shard_map/ppermute | solution.py:220
  155.3 5.4 %copy-start.6 = (bf16[1024,768]{1,0:T(8,128)(2,1)}, bf16[1024,768]{1,0:T(8,128)(2,1)S(1)}, u32[]{:S(2)}) copy-start(bf16[1024,768]{1,0:T(8,128)(2,1)S(1)} %collective-permute-done.4.refs_1_) | copy-start | bytes 4718596
  157.8 3.0 %copy-start.8 = (bf16[1024,768]{1,0:T(8,128)(2,1)}, bf16[1024,768]{1,0:T(8,128)(2,1)S(1)}, u32[]{:S(2)}) copy-start(bf16[1024,768]{1,0:T(8,128)(2,1)S(1)} %collective-permute-done.5.refs_2_) | copy-start | bytes 4718596
  160.8 0.8 copy-start.17
  161.6 22.0 %collective-permute-start.11 = (bf16[512,768]{1,0:T(8,128)(2,1)}, bf16[512,768]{1,0:T(8,128)(2,1)}, u32[]{:S(2)}, u32[]{:S(2)}) collective-permute-start(bf16[512,768]{1,0:T(8,128)(2,1)} %get-tuple-element.81), channel_id=1, source_target_pairs={{0,6},{1,7},{2,4},{3,5},{4,2},{5,3},{6,0},{7,1},{8,14},{9,15},{10,... | collective-permute-start | bytes 2359304 | tf_op jit(solution)/shard_map/ppermute | solution.py:220
  163.7 20.8 %collective-permute-start.12 = (bf16[512,768]{1,0:T(8,128)(2,1)}, bf16[512,768]{1,0:T(8,128)(2,1)}, u32[]{:S(2)}, u32[]{:S(2)}) collective-permute-start(bf16[512,768]{1,0:T(8,128)(2,1)} %get-tuple-element.82), channel_id=1, source_target_pairs={{0,2},{1,3},{2,0},{3,1},{4,6},{5,7},{6,4},{7,5},{8,10},{9,11},{10,... | collective-permute-start | bytes 2359304 | tf_op jit(solution)/shard_map/ppermute | solution.py:220
  163.7 20.8 %copy-start.5 = (bf16[768,1536]{1,0:T(8,128)(2,1)S(1)}, bf16[768,1536]{1,0:T(8,128)(2,1)}, u32[]{:S(2)}) copy-start(bf16[768,1536]{1,0:T(8,128)(2,1)} %copy-done.4) | copy-start | bytes 7077892
  163.7 20.8 %copy-start.7 = (bf16[1024,768]{1,0:T(8,128)(2,1)S(1)}, bf16[1024,768]{1,0:T(8,128)(2,1)}, u32[]{:S(2)}) copy-start(bf16[1024,768]{1,0:T(8,128)(2,1)} %copy-done.6) | copy-start | bytes 4718596
  168.5 37.3 %collective-permute-start.8 = (bf16[1024,512]{1,0:T(8,128)(2,1)S(1)}, bf16[1024,512]{1,0:T(8,128)(2,1)S(1)}, u32[]{:S(2)}, u32[]{:S(2)}) collective-permute-start(bf16[1024,512]{1,0:T(8,128)(2,1)S(1)} %get-tuple-element.78), channel_id=1, source_target_pairs={{0,2},{1,3},{2,0},{3,1},{4,6},{5,7},{6,4},{7,5},{8,10},{9,11},{10,... | collective-permute-start | bytes 3145736 | tf_op jit(solution)/shard_map/ppermute | solution.py:220
  170.6 35.2 %collective-permute-start.9 = (bf16[1024,512]{1,0:T(8,128)(2,1)S(1)}, bf16[1024,512]{1,0:T(8,128)(2,1)S(1)}, u32[]{:S(2)}, u32[]{:S(2)}) collective-permute-start(bf16[1024,512]{1,0:T(8,128)(2,1)S(1)} %get-tuple-element.79), channel_id=1, source_target_pairs={{0,6},{1,7},{2,4},{3,5},{4,2},{5,3},{6,0},{7,1},{8,14},{9,15},{10,... | collective-permute-start | bytes 3145736 | tf_op jit(solution)/shard_map/ppermute | solution.py:220
  171.6 34.2 %collective-permute-start.10 = (bf16[1024,256]{1,0:T(8,128)(2,1)S(1)}, bf16[1024,256]{1,0:T(8,128)(2,1)S(1)}, u32[]{:S(2)}, u32[]{:S(2)}) collective-permute-start(bf16[1024,256]{1,0:T(8,128)(2,1)S(1)} %get-tuple-element.80), channel_id=1, source_target_pairs={{0,1},{1,0},{2,3},{3,2},{4,5},{5,4},{6,7},{7,6},{8,9},{9,8},{10,11... | collective-permute-start | bytes 1572872 | tf_op jit(solution)/shard_map/ppermute | solution.py:220
  184.5 1.4 copy-start.9
  188.9 12.7 %collective-permute-start.13 = (bf16[256,768]{1,0:T(8,128)(2,1)S(1)}, bf16[256,768]{1,0:T(8,128)(2,1)S(1)}, u32[]{:S(2)}, u32[]{:S(2)}) collective-permute-start(bf16[256,768]{1,0:T(8,128)(2,1)S(1)} %get-tuple-element.86), channel_id=1, source_target_pairs={{0,1},{1,0},{2,3},{3,2},{4,5},{5,4},{6,7},{7,6},{8,9},{9,8},{10,11... | collective-permute-start | bytes 1179656 | tf_op jit(solution)/shard_map/ppermute | solution.py:220
  191.9 13.9 %collective-permute-start.14 = (bf16[256,768]{1,0:T(8,128)(2,1)S(1)}, bf16[256,768]{1,0:T(8,128)(2,1)S(1)}, u32[]{:S(2)}, u32[]{:S(2)}) collective-permute-start(bf16[256,768]{1,0:T(8,128)(2,1)S(1)} %get-tuple-element.87), channel_id=1, source_target_pairs={{0,1},{1,0},{2,3},{3,2},{4,5},{5,4},{6,7},{7,6},{8,9},{9,8},{10,11... | collective-permute-start | bytes 1179656 | tf_op jit(solution)/shard_map/ppermute | solution.py:220
  207.9 11.9 %collective-permute-start.15 = (bf16[512,512]{1,0:T(8,128)(2,1)S(1)}, bf16[512,512]{1,0:T(8,128)(2,1)S(1)}, u32[]{:S(2)}, u32[]{:S(2)}) collective-permute-start(bf16[512,512]{1,0:T(8,128)(2,1)S(1)} %get-tuple-element.89), channel_id=1, source_target_pairs={{0,6},{1,7},{2,4},{3,5},{4,2},{5,3},{6,0},{7,1},{8,14},{9,15},{10,... | collective-permute-start | bytes 1572872 | tf_op jit(solution)/shard_map/ppermute | solution.py:220
  209.8 11.8 %collective-permute-start.16 = (bf16[512,512]{1,0:T(8,128)(2,1)S(1)}, bf16[512,512]{1,0:T(8,128)(2,1)S(1)}, u32[]{:S(2)}, u32[]{:S(2)}) collective-permute-start(bf16[512,512]{1,0:T(8,128)(2,1)S(1)} %get-tuple-element.90), channel_id=1, source_target_pairs={{0,1},{1,0},{2,3},{3,2},{4,5},{5,4},{6,7},{7,6},{8,9},{9,8},{10,11... | collective-permute-start | bytes 1572872 | tf_op jit(solution)/shard_map/ppermute | solution.py:220
  212.5 6.4 %collective-permute-start.17 = (bf16[512,256]{1,0:T(8,128)(2,1)S(1)}, bf16[512,256]{1,0:T(8,128)(2,1)S(1)}, u32[]{:S(2)}, u32[]{:S(2)}) collective-permute-start(bf16[512,256]{1,0:T(8,128)(2,1)S(1)} %get-tuple-element.91), channel_id=1, source_target_pairs={{0,2},{1,3},{2,0},{3,1},{4,6},{5,7},{6,4},{7,5},{8,10},{9,11},{10,... | collective-permute-start | bytes 786440 | tf_op jit(solution)/shard_map/ppermute | solution.py:220
  221.6 11.2 %copy-start.18 = (bf16[256,768]{1,0:T(8,128)(2,1)S(1)}, bf16[256,768]{1,0:T(8,128)(2,1)}, u32[]{:S(2)}) copy-start(bf16[256,768]{1,0:T(8,128)(2,1)} %copy-done.17) | copy-start | bytes 1179652
  223.5 9.0 %collective-permute-start.18 = (bf16[256,512]{1,0:T(8,128)(2,1)S(1)}, bf16[256,512]{1,0:T(8,128)(2,1)S(1)}, u32[]{:S(2)}, u32[]{:S(2)}) collective-permute-start(bf16[256,512]{1,0:T(8,128)(2,1)S(1)} %get-tuple-element.96), channel_id=1, source_target_pairs={{0,1},{1,0},{2,3},{3,2},{4,5},{5,4},{6,7},{7,6},{8,9},{9,8},{10,11... | collective-permute-start | bytes 786440 | tf_op jit(solution)/shard_map/ppermute | solution.py:220
  226.4 6.4 %collective-permute-start.19 = (bf16[256,512]{1,0:T(8,128)(2,1)S(1)}, bf16[256,512]{1,0:T(8,128)(2,1)S(1)}, u32[]{:S(2)}, u32[]{:S(2)}) collective-permute-start(bf16[256,512]{1,0:T(8,128)(2,1)S(1)} %get-tuple-element.97), channel_id=1, source_target_pairs={{0,2},{1,3},{2,0},{3,1},{4,6},{5,7},{6,4},{7,5},{8,10},{9,11},{10,... | collective-permute-start | bytes 786440 | tf_op jit(solution)/shard_map/ppermute | solution.py:220
  226.4 6.2 %collective-permute-start.20 = (bf16[256,256]{1,0:T(8,128)(2,1)S(1)}, bf16[256,256]{1,0:T(8,128)(2,1)S(1)}, u32[]{:S(2)}, u32[]{:S(2)}) collective-permute-start(bf16[256,256]{1,0:T(8,128)(2,1)S(1)} %get-tuple-element.98), channel_id=1, source_target_pairs={{0,6},{1,7},{2,4},{3,5},{4,2},{5,3},{6,0},{7,1},{8,14},{9,15},{10,... | collective-permute-start | bytes 393224 | tf_op jit(solution)/shard_map/ppermute | solution.py:220
  (3 other events, 2.0 us)

commit v5 on v4

--- a/solution.py
+++ b/solution.py
@@ -30,7 +30,7 @@
 )
 
 
-def rows_kernel(columns, capacity, start, routes_ref, probs_ref, grad_ref, token_ref, out_ref, _):
+def rows_kernel(columns, capacity, routes_ref, probs_ref, grad_ref, token_ref, out_ref, _):
     top, tok = routes_ref.shape
     ids = lax.broadcasted_iota(jnp.int32, (columns, tok), 0) * EXP_DEV
     named = jnp.zeros((columns, tok), jnp.float32)
@@ -49,8 +49,7 @@
     weight = jnp.sum(jnp.where(pick, prob[:, None, :], 0.0), axis=2, keepdims=True)
     weight = weight.reshape(columns * capacity, 1)
     pick = jnp.where(pick, 1.0, 0.0).reshape(columns * capacity, tok).astype(jnp.bfloat16)
-    width = out_ref.shape[1]
-    taken = jnp.dot(pick, grad_ref[:, start : start + width], preferred_element_type=jnp.float32)
+    taken = jnp.dot(pick, grad_ref[...], preferred_element_type=jnp.float32)
     out_ref[...] = (weight * taken).astype(jnp.bfloat16)
 
 
@@ -186,13 +185,13 @@
             width = sum(WIDTHS[c])
             start = sum(sum(w) for w in WIDTHS[:c])
             rows, token = pl.pallas_call(
-                functools.partial(rows_kernel, ranks, capacity, start),
+                functools.partial(rows_kernel, ranks, capacity),
                 in_specs=[vmem] * 3 + [anywhere],
                 out_specs=[vmem, anywhere],
                 out_shape=[shape(slot_count, width), jax.ShapeDtypeStruct(token.shape, token.dtype)],
                 input_output_aliases={3: 1},
                 compiler_params=pltpu.CompilerParams(vmem_limit_bytes=VMEM),
-            )(routes.T, route_probs.T, grad_out, token)
+            )(routes.T, route_probs.T, grad_out[:, start : start + width], token)
             rows = rows.reshape(ranks, capacity, width)
             rows = lax.all_to_all(rows, "ep", split_axis=0, concat_axis=0, tiled=True)
             arrived[c], came[c] = rows.reshape(slot_count, width), []

time: 235 us -> 235 us (level)
    slice x0 -> x3, local copies, waits for them, and re-layouts: none -> 3.15 us  [shards(): grad_out[:, start:start + width]]
    unnamed x54 -> x48, local copies, waits for them, and re-layouts: 13.1 us -> 10.7 us
  transfers between devices with their start and end apart: 24 -> 24, of which waited for: 19 -> 19; matrix products, arithmetic and copies ran while one was open for 0% -> 1% of each run, Pallas kernels for 10% -> 10%
where the time goes in v5:
time: 235 us
  waiting for transfers between devices  134 us (57%)
  starting transfers between devices  55.7 us (24%)
  Pallas kernels  30.9 us (13%)
  local copies, waits for them, and re-layouts  13.9 us (6%)
    ppermute x21, waiting for transfers between devices, shards(): lax.ppermute(m, 'dp', partners[order[kind - 1]])  96 us
    all_to_all x3, waiting for transfers between devices, shards(): rows = lax.all_to_all(rows, 'ep', split_axis=0, concat_axis=0, tiled=True)  37.6 us
    ppermute x21, starting transfers between devices, shards(): lax.ppermute(m, 'dp', partners[order[kind - 1]])  34.2 us
    pallas_call x10, Pallas kernels, step(): pl.pallas_call(functools.partial(step_kernel, size, counts), in_specs=[pl...  27.4 us
    all_to_all x3, starting transfers between devices, shards(): rows = lax.all_to_all(rows, 'ep', split_axis=0, concat_axis=0, tiled=True)  21.5 us
    unnamed x48, local copies, waits for them, and re-layouts  10.7 us
  transfers between devices with their start and end apart: 24, of which 19 were waited for; matrix products, arithmetic and copies ran while one was open for 1% of the time, Pallas kernels for 10%

profile of v5, /device:TPU:32, one launch (start us, length us, event | category | flops | bytes accessed | tf_op | source)
XLA Modules:
  0.0 234.7 jit_solution(7696794713576000005)
XLA Ops:
  2.4 1.7 shard_map.46
  4.1 9.8 %all-to-all-start = ((bf16[32,24,768]{2,1,0:T(8,128)(2,1)}), bf16[32,24,768]{2,1,0:T(8,128)(2,1)S(1)}, u32[]{:S(2)}, u32[]{:S(2)}) async-start(bf16[32,24,768]{2,1,0:T(8,128)(2,1)} %bitcast.5), calls=%async_computation | async-start | bytes 2359296 | tf_op jit(solution)/shard_map/all_to_all | solution.py:196
  13.9 1.1 slice.11.grad_ref
  16.0 1.4 copy-done.9
  17.4 27.3 %all-to-all-done = bf16[32,24,768]{2,1,0:T(8,128)(2,1)S(1)} async-done(((bf16[32,24,768]{2,1,0:T(8,128)(2,1)}), bf16[32,24,768]{2,1,0:T(8,128)(2,1)S(1)}, u32[]{:S(2)}, u32[]{:S(2)}) %all-to-all-start) | async-done | bytes 1179680 | tf_op jit(solution)/shard_map/all_to_all | solution.py:196
  45.7 5.9 %all-to-all-start.2 = ((bf16[32,24,1536]{2,1,0:T(8,128)(2,1)}), bf16[32,24,1536]{2,1,0:T(8,128)(2,1)}, u32[]{:S(2)}, u32[]{:S(2)}) async-start(bf16[32,24,1536]{2,1,0:T(8,128)(2,1)} %bitcast.22), calls=%async_computation.2 | async-start | bytes 4718592 | tf_op jit(solution)/shard_map/all_to_all | solution.py:196
  51.8 1.3 copy-done.8
  53.1 2.8 %shard_map.48 = (bf16[1024,384]{1,0:T(8,128)(2,1)S(1)}, bf16[1024,384]{1,0:T(8,128)(2,1)S(1)}, bf16[768,768]{1,0:T(8,128)(2,1)S(1)}, s32[8,128]{1,0:T(8,128)S(1)}) custom-call(s32[2]{0:T(128)S(1)} %pad_add_fusion.place_ref, bf16[768,2048]{1,0:T(8,128)(2,1)S(1)} %bitcast.11, bf16[768,768]{1,0:T(8,128)(2,1)S(1)} %bitcast.21, ...), custom_call_target="tpu_custom_call", output_to_operand_aliasing={{3}: (3, {})} | custom-call | tf_op jit(solution)/shard_map/pallas_call | solution.py:143
  55.9 1.7 collective-permute-start
  57.5 2.2 collective-permute-start.1
  59.7 15.8 %collective-permute-done.refs_1_ = bf16[1024,384]{1,0:T(8,128)(2,1)S(1)} collective-permute-done((bf16[1024,384]{1,0:T(8,128)(2,1)S(1)}, bf16[1024,384]{1,0:T(8,128)(2,1)S(1)}, u32[]{:S(2)}, u32[]{:S(2)}) %collective-permute-start) | collective-permute-done | bytes 786464 | tf_op jit(solution)/shard_map/ppermute | solution.py:219
  75.6 2.5 %collective-permute-done.1.refs_2_ = bf16[1024,384]{1,0:T(8,128)(2,1)S(1)} collective-permute-done((bf16[1024,384]{1,0:T(8,128)(2,1)S(1)}, bf16[1024,384]{1,0:T(8,128)(2,1)S(1)}, u32[]{:S(2)}, u32[]{:S(2)}) %collective-permute-start.1) | collective-permute-done | bytes 786464 | tf_op jit(solution)/shard_map/ppermute | solution.py:219
  78.1 1.6 shard_map.49
  79.7 2.2 collective-permute-start.2
  83.0 8.1 %collective-permute-done.2.refs_3_ = bf16[512,384]{1,0:T(8,128)(2,1)S(1)} collective-permute-done((bf16[512,384]{1,0:T(8,128)(2,1)S(1)}, bf16[512,384]{1,0:T(8,128)(2,1)S(1)}, u32[]{:S(2)}, u32[]{:S(2)}) %collective-permute-start.2) | collective-permute-done | bytes 393248 | tf_op jit(solution)/shard_map/ppermute | solution.py:219
  91.8 1.6 shard_map.50
  96.4 1.3 copy-done.10
  97.7 10.3 %all-to-all-done.2 = bf16[32,24,1536]{2,1,0:T(8,128)(2,1)} async-done(((bf16[32,24,1536]{2,1,0:T(8,128)(2,1)}), bf16[32,24,1536]{2,1,0:T(8,128)(2,1)}, u32[]{:S(2)}, u32[]{:S(2)}) %all-to-all-start.2) | async-done | bytes 2359328 | tf_op jit(solution)/shard_map/all_to_all | solution.py:196
  108.0 5.8 %all-to-all-start.1 = ((bf16[32,24,1280]{2,1,0:T(8,128)(2,1)}), bf16[32,24,1280]{2,1,0:T(8,128)(2,1)}, u32[]{:S(2)}, u32[]{:S(2)}) async-start(bf16[32,24,1280]{2,1,0:T(8,128)(2,1)} %bitcast.23), calls=%async_computation.1 | async-start | bytes 3932160 | tf_op jit(solution)/shard_map/all_to_all | solution.py:196
  113.8 4.8 %shard_map.52 = (bf16[1024,768]{1,0:T(8,128)(2,1)S(1)}, bf16[1024,768]{1,0:T(8,128)(2,1)S(1)}, bf16[768,1536]{1,0:T(8,128)(2,1)S(1)}, s32[8,128]{1,0:T(8,128)S(1)}) custom-call(s32[2]{0:T(128)S(1)} %pad_add_fusion.place_ref, bf16[768,2048]{1,0:T(8,128)(2,1)S(1)} %bitcast.14, bf16[768,1536]{1,0:T(8,128)(2,1)} %bitcast.10.refs_0_, ...), custom_call_target="tpu_custom_call", output_to_operand_aliasing={{3}: (3, {})} | custom-call | tf_op jit(solution)/shard_map/pallas_call | solution.py:143
  118.6 1.7 collective-permute-start.4
  120.2 2.2 collective-permute-start.5
  122.4 2.7 %collective-permute-start.6 = (bf16[256,384]{1,0:T(8,128)(2,1)S(1)}, bf16[256,384]{1,0:T(8,128)(2,1)S(1)}, u32[]{:S(2)}, u32[]{:S(2)}) collective-permute-start(bf16[256,384]{1,0:T(8,128)(2,1)S(1)} %copy-done.23), channel_id=1, source_target_pairs={{0,1},{1,0},{2,3},{3,2},{4,5},{5,4},{6,7},{7,6},{8,9},{9,8},{10,11... | collective-permute-start | bytes 589832 | tf_op jit(solution)/shard_map/ppermute | solution.py:219
  125.9 11.8 %collective-permute-done.6.refs_5_ = bf16[256,384]{1,0:T(8,128)(2,1)S(1)} collective-permute-done((bf16[256,384]{1,0:T(8,128)(2,1)S(1)}, bf16[256,384]{1,0:T(8,128)(2,1)S(1)}, u32[]{:S(2)}, u32[]{:S(2)}) %collective-permute-start.6) | collective-permute-done | bytes 196640 | tf_op jit(solution)/shard_map/ppermute | solution.py:219
  137.7 4.1 %collective-permute-done.7.refs_6_ = bf16[256,384]{1,0:T(8,128)(2,1)S(1)} collective-permute-done((bf16[256,384]{1,0:T(8,128)(2,1)S(1)}, bf16[256,384]{1,0:T(8,128)(2,1)S(1)}, u32[]{:S(2)}, u32[]{:S(2)}) %collective-permute-start.7) | collective-permute-done | bytes 196640 | tf_op jit(solution)/shard_map/ppermute | solution.py:219
  141.8 13.3 %collective-permute-done.4.refs_1_ = bf16[1024,768]{1,0:T(8,128)(2,1)S(1)} collective-permute-done((bf16[1024,768]{1,0:T(8,128)(2,1)S(1)}, bf16[1024,768]{1,0:T(8,128)(2,1)S(1)}, u32[]{:S(2)}, u32[]{:S(2)}) %collective-permute-start.4) | collective-permute-done | bytes 1572896 | tf_op jit(solution)/shard_map/ppermute | solution.py:219
  155.1 2.5 %collective-permute-done.5.refs_2_ = bf16[1024,768]{1,0:T(8,128)(2,1)S(1)} collective-permute-done((bf16[1024,768]{1,0:T(8,128)(2,1)S(1)}, bf16[1024,768]{1,0:T(8,128)(2,1)S(1)}, u32[]{:S(2)}, u32[]{:S(2)}) %collective-permute-start.5) | collective-permute-done | bytes 1572896 | tf_op jit(solution)/shard_map/ppermute | solution.py:219
  157.6 2.9 %shard_map.53 = (bf16[512,768]{1,0:T(8,128)(2,1)}, bf16[512,768]{1,0:T(8,128)(2,1)}, bf16[256,768]{1,0:T(8,128)(2,1)S(1)}, s32[8,128]{1,0:T(8,128)S(1)}) custom-call(s32[2]{0:T(128)S(1)} %pad_add_fusion.place_ref, bf16[768,2048]{1,0:T(8,128)(2,1)S(1)} %bitcast.15, bf16[768,1536]{1,0:T(8,128)(2,1)S(1)} %get-tuple-element.68.refs_0_, ...), custom_call_target="tpu_custom_call", output_to_operand_aliasing={{3}: (9, {})} | custom-call | tf_op jit(solution)/shard_map/pallas_call | solution.py:143
  161.3 2.2 collective-permute-start.11
  163.5 4.7 %shard_map.54 = (bf16[1024,512]{1,0:T(8,128)(2,1)S(1)}, bf16[1024,512]{1,0:T(8,128)(2,1)S(1)}, bf16[1024,256]{1,0:T(8,128)(2,1)S(1)}, bf16[768,1280]{1,0:T(8,128)(2,1)S(1)}, s32[8,128]{1,0:T(8,128)S(1)}) custom-call(s32[2]{0:T(128)S(1)} %pad_add_fusion.place_ref, bf16[768,2048]{1,0:T(8,128)(2,1)S(1)} %bitcast.16, ...), custom_call_target="tpu_custom_call", output_to_operand_aliasing={{4}: (3, {})} | custom-call | tf_op jit(solution)/shard_map/pallas_call | solution.py:143
  168.3 2.1 collective-permute-start.8
  171.4 2.7 %collective-permute-start.10 = (bf16[1024,256]{1,0:T(8,128)(2,1)S(1)}, bf16[1024,256]{1,0:T(8,128)(2,1)S(1)}, u32[]{:S(2)}, u32[]{:S(2)}) collective-permute-start(bf16[1024,256]{1,0:T(8,128)(2,1)S(1)} %get-tuple-element.80), channel_id=1, source_target_pairs={{0,1},{1,0},{2,3},{3,2},{4,5},{5,4},{6,7},{7,6},{8,9},{9,8},{10,11... | collective-permute-start | bytes 1572872 | tf_op jit(solution)/shard_map/ppermute | solution.py:219
  174.1 9.2 %collective-permute-done.11.refs_3_ = bf16[512,768]{1,0:T(8,128)(2,1)} collective-permute-done((bf16[512,768]{1,0:T(8,128)(2,1)}, bf16[512,768]{1,0:T(8,128)(2,1)}, u32[]{:S(2)}, u32[]{:S(2)}) %collective-permute-start.11) | collective-permute-done | bytes 786464 | tf_op jit(solution)/shard_map/ppermute | solution.py:219
  184.3 1.4 copy-done.6
  185.7 2.9 %shard_map.55 = (bf16[256,768]{1,0:T(8,128)(2,1)S(1)}, bf16[256,768]{1,0:T(8,128)(2,1)S(1)}, f32[256,768]{1,0:T(8,128)S(1)}, f32[256,768]{1,0:T(8,128)S(1)}, s32[8,128]{1,0:T(8,128)S(1)}) custom-call(s32[2]{0:T(128)S(1)} %pad_add_fusion.place_ref, bf16[768,2048]{1,0:T(8,128)(2,1)S(1)} %bitcast.17, ...), custom_call_target="tpu_custom_call", output_to_operand_aliasing={{4}: (7, {})} | custom-call | tf_op jit(solution)/shard_map/pallas_call | solution.py:143
  188.7 3.0 %collective-permute-start.13 = (bf16[256,768]{1,0:T(8,128)(2,1)S(1)}, bf16[256,768]{1,0:T(8,128)(2,1)S(1)}, u32[]{:S(2)}, u32[]{:S(2)}) collective-permute-start(bf16[256,768]{1,0:T(8,128)(2,1)S(1)} %get-tuple-element.86), channel_id=1, source_target_pairs={{0,1},{1,0},{2,3},{3,2},{4,5},{5,4},{6,7},{7,6},{8,9},{9,8},{10,11... | collective-permute-start | bytes 1179656 | tf_op jit(solution)/shard_map/ppermute | solution.py:219
  192.5 8.9 %collective-permute-done.13.refs_6_ = bf16[256,768]{1,0:T(8,128)(2,1)S(1)} collective-permute-done((bf16[256,768]{1,0:T(8,128)(2,1)S(1)}, bf16[256,768]{1,0:T(8,128)(2,1)S(1)}, u32[]{:S(2)}, u32[]{:S(2)}) %collective-permute-start.13) | collective-permute-done | bytes 393248 | tf_op jit(solution)/shard_map/ppermute | solution.py:219
  201.4 4.2 %collective-permute-done.14.refs_7_ = bf16[256,768]{1,0:T(8,128)(2,1)S(1)} collective-permute-done((bf16[256,768]{1,0:T(8,128)(2,1)S(1)}, bf16[256,768]{1,0:T(8,128)(2,1)S(1)}, u32[]{:S(2)}, u32[]{:S(2)}) %collective-permute-start.14) | collective-permute-done | bytes 393248 | tf_op jit(solution)/shard_map/ppermute | solution.py:219
  205.6 2.1 shard_map.56
  207.7 1.8 collective-permute-start.15
  209.6 2.7 %collective-permute-start.16 = (bf16[512,512]{1,0:T(8,128)(2,1)S(1)}, bf16[512,512]{1,0:T(8,128)(2,1)S(1)}, u32[]{:S(2)}, u32[]{:S(2)}) collective-permute-start(bf16[512,512]{1,0:T(8,128)(2,1)S(1)} %get-tuple-element.90), channel_id=1, source_target_pairs={{0,1},{1,0},{2,3},{3,2},{4,5},{5,4},{6,7},{7,6},{8,9},{9,8},{10,11... | collective-permute-start | bytes 1572872 | tf_op jit(solution)/shard_map/ppermute | solution.py:219
  212.3 6.4 %collective-permute-done.17.refs_6_ = bf16[512,256]{1,0:T(8,128)(2,1)S(1)} collective-permute-done((bf16[512,256]{1,0:T(8,128)(2,1)S(1)}, bf16[512,256]{1,0:T(8,128)(2,1)S(1)}, u32[]{:S(2)}, u32[]{:S(2)}) %collective-permute-start.17) | collective-permute-done | bytes 262176 | tf_op jit(solution)/shard_map/ppermute | solution.py:219
  219.6 1.8 collective-permute-done.16.refs_5_
  221.4 2.0 shard_map.57
  223.3 2.8 %collective-permute-start.18 = (bf16[256,512]{1,0:T(8,128)(2,1)S(1)}, bf16[256,512]{1,0:T(8,128)(2,1)S(1)}, u32[]{:S(2)}, u32[]{:S(2)}) collective-permute-start(bf16[256,512]{1,0:T(8,128)(2,1)S(1)} %get-tuple-element.96), channel_id=1, source_target_pairs={{0,1},{1,0},{2,3},{3,2},{4,5},{5,4},{6,7},{7,6},{8,9},{9,8},{10,11... | collective-permute-start | bytes 786440 | tf_op jit(solution)/shard_map/ppermute | solution.py:219
  226.2 1.5 collective-permute-start.20
  227.7 4.7 %collective-permute-done.20.refs_5_ = bf16[256,256]{1,0:T(8,128)(2,1)S(1)} collective-permute-done((bf16[256,256]{1,0:T(8,128)(2,1)S(1)}, bf16[256,256]{1,0:T(8,128)(2,1)S(1)}, u32[]{:S(2)}, u32[]{:S(2)}) %collective-permute-start.20) | collective-permute-done | bytes 131104 | tf_op jit(solution)/shard_map/ppermute | solution.py:219
  232.5 2.0 shard_map.58
  (66 shorter events, 14.7 us)
Async XLA Ops:
  1.0 0.7 copy-start.15
  1.7 0.7 copy-start.17
  4.1 10.9 %copy-start.16 = (s32[192,8]{0,1:T(8,128)S(1)}, s32[192,8]{0,1:T(8,128)}, u32[]{:S(2)}) copy-start(s32[192,8]{0,1:T(8,128)} %param.6) | copy-start | bytes 18436
  4.1 10.9 %copy-start.18 = (f32[192,8]{0,1:T(8,128)S(1)}, f32[192,8]{0,1:T(8,128)}, u32[]{:S(2)}) copy-start(f32[192,8]{0,1:T(8,128)} %param.5) | copy-start | bytes 18436
  4.1 40.7 %all-to-all-start = ((bf16[32,24,768]{2,1,0:T(8,128)(2,1)}), bf16[32,24,768]{2,1,0:T(8,128)(2,1)S(1)}, u32[]{:S(2)}, u32[]{:S(2)}) async-start(bf16[32,24,768]{2,1,0:T(8,128)(2,1)} %bitcast.5), calls=%async_computation | async-start | bytes 2359296 | tf_op jit(solution)/shard_map/all_to_all | solution.py:196
  16.0 1.5 copy-start.9
  44.7 1.0 copy-start.7
  45.7 6.1 %copy-start = (bf16[1,768,2048]{2,1,0:T(8,128)(2,1)S(1)}, bf16[1,768,2048]{2,1,0:T(8,128)(2,1)}, u32[]{:S(2)}) copy-start(bf16[1,768,2048]{2,1,0:T(8,128)(2,1)} %param.7) | copy-start | bytes 9437188
  45.7 62.2 %all-to-all-start.2 = ((bf16[32,24,1536]{2,1,0:T(8,128)(2,1)}), bf16[32,24,1536]{2,1,0:T(8,128)(2,1)}, u32[]{:S(2)}, u32[]{:S(2)}) async-start(bf16[32,24,1536]{2,1,0:T(8,128)(2,1)} %bitcast.22), calls=%async_computation.2 | async-start | bytes 4718592 | tf_op jit(solution)/shard_map/all_to_all | solution.py:196
  51.8 1.3 copy-start.8
  55.9 19.7 %collective-permute-start = (bf16[1024,384]{1,0:T(8,128)(2,1)S(1)}, bf16[1024,384]{1,0:T(8,128)(2,1)S(1)}, u32[]{:S(2)}, u32[]{:S(2)}) collective-permute-start(bf16[1024,384]{1,0:T(8,128)(2,1)S(1)} %get-tuple-element.58), channel_id=1, source_target_pairs={{0,2},{1,3},{2,0},{3,1},{4,6},{5,7},{6,4},{7,5},{8,10},{9,11},{10,... | collective-permute-start | bytes 2359304 | tf_op jit(solution)/shard_map/ppermute | solution.py:219
  57.5 20.5 %collective-permute-start.1 = (bf16[1024,384]{1,0:T(8,128)(2,1)S(1)}, bf16[1024,384]{1,0:T(8,128)(2,1)S(1)}, u32[]{:S(2)}, u32[]{:S(2)}) collective-permute-start(bf16[1024,384]{1,0:T(8,128)(2,1)S(1)} %get-tuple-element.59), channel_id=1, source_target_pairs={{0,6},{1,7},{2,4},{3,5},{4,2},{5,3},{6,0},{7,1},{8,14},{9,15},{10,... | collective-permute-start | bytes 2359304 | tf_op jit(solution)/shard_map/ppermute | solution.py:219
  79.7 11.4 %collective-permute-start.2 = (bf16[512,384]{1,0:T(8,128)(2,1)S(1)}, bf16[512,384]{1,0:T(8,128)(2,1)S(1)}, u32[]{:S(2)}, u32[]{:S(2)}) collective-permute-start(bf16[512,384]{1,0:T(8,128)(2,1)S(1)} %get-tuple-element.61), channel_id=1, source_target_pairs={{0,6},{1,7},{2,4},{3,5},{4,2},{5,3},{6,0},{7,1},{8,14},{9,15},{10,... | collective-permute-start | bytes 1179656 | tf_op jit(solution)/shard_map/ppermute | solution.py:219
  82.0 9.8 %collective-permute-start.3 = (bf16[512,384]{1,0:T(8,128)(2,1)S(1)}, bf16[512,384]{1,0:T(8,128)(2,1)S(1)}, u32[]{:S(2)}, u32[]{:S(2)}) collective-permute-start(bf16[512,384]{1,0:T(8,128)(2,1)S(1)} %get-tuple-element.62), channel_id=1, source_target_pairs={{0,2},{1,3},{2,0},{3,1},{4,6},{5,7},{6,4},{7,5},{8,10},{9,11},{10,... | collective-permute-start | bytes 1179656 | tf_op jit(solution)/shard_map/ppermute | solution.py:219
  91.8 3.7 %copy-start.19 = (f32[192,8]{0,1:T(8,128)S(1)}, f32[192,8]{0,1:T(8,128)}, u32[]{:S(2)}) copy-start(f32[192,8]{0,1:T(8,128)} %param.5) | copy-start | bytes 18436
  93.4 0.8 copy-start.11
  94.2 0.7 copy-start.20
  94.9 0.7 copy-start.22
  96.4 1.3 copy-start.10
  108.0 55.5 %all-to-all-start.1 = ((bf16[32,24,1280]{2,1,0:T(8,128)(2,1)}), bf16[32,24,1280]{2,1,0:T(8,128)(2,1)}, u32[]{:S(2)}, u32[]{:S(2)}) async-start(bf16[32,24,1280]{2,1,0:T(8,128)(2,1)} %bitcast.23), calls=%async_computation.1 | async-start | bytes 3932160 | tf_op jit(solution)/shard_map/all_to_all | solution.py:196
  113.8 8.6 %copy-start.23 = (bf16[256,384]{1,0:T(8,128)(2,1)S(1)}, bf16[256,384]{1,0:T(8,128)(2,1)}, u32[]{:S(2)}) copy-start(bf16[256,384]{1,0:T(8,128)(2,1)} %copy-done.22) | copy-start | bytes 589828
  113.8 11.4 %copy-start.21 = (bf16[256,384]{1,0:T(8,128)(2,1)S(1)}, bf16[256,384]{1,0:T(8,128)(2,1)}, u32[]{:S(2)}) copy-start(bf16[256,384]{1,0:T(8,128)(2,1)} %copy-done.20) | copy-start | bytes 589828
  113.8 43.8 %copy-start.12 = (f32[256,384]{1,0:T(8,128)S(1)}, f32[256,384]{1,0:T(8,128)}, u32[]{:S(2)}) copy-start(f32[256,384]{1,0:T(8,128)} %copy-done.11) | copy-start | bytes 1179652
  118.6 42.0 %copy-start.1 = (bf16[768,1536]{1,0:T(8,128)(2,1)}, bf16[768,1536]{1,0:T(8,128)(2,1)S(1)}, u32[]{:S(2)}) copy-start(bf16[768,1536]{1,0:T(8,128)(2,1)S(1)} %get-tuple-element.68.refs_0_) | copy-start | bytes 7077892
  118.6 36.5 %collective-permute-start.4 = (bf16[1024,768]{1,0:T(8,128)(2,1)S(1)}, bf16[1024,768]{1,0:T(8,128)(2,1)S(1)}, u32[]{:S(2)}, u32[]{:S(2)}) collective-permute-start(bf16[1024,768]{1,0:T(8,128)(2,1)S(1)} %get-tuple-element.69), channel_id=1, source_target_pairs={{0,2},{1,3},{2,0},{3,1},{4,6},{5,7},{6,4},{7,5},{8,10},{9,11},{10,... | collective-permute-start | bytes 4718600 | tf_op jit(solution)/shard_map/ppermute | solution.py:219
  120.2 37.4 %collective-permute-start.5 = (bf16[1024,768]{1,0:T(8,128)(2,1)S(1)}, bf16[1024,768]{1,0:T(8,128)(2,1)S(1)}, u32[]{:S(2)}, u32[]{:S(2)}) collective-permute-start(bf16[1024,768]{1,0:T(8,128)(2,1)S(1)} %get-tuple-element.70), channel_id=1, source_target_pairs={{0,6},{1,7},{2,4},{3,5},{4,2},{5,3},{6,0},{7,1},{8,14},{9,15},{10,... | collective-permute-start | bytes 4718600 | tf_op jit(solution)/shard_map/ppermute | solution.py:219
  122.4 15.3 %collective-permute-start.6 = (bf16[256,384]{1,0:T(8,128)(2,1)S(1)}, bf16[256,384]{1,0:T(8,128)(2,1)S(1)}, u32[]{:S(2)}, u32[]{:S(2)}) collective-permute-start(bf16[256,384]{1,0:T(8,128)(2,1)S(1)} %copy-done.23), channel_id=1, source_target_pairs={{0,1},{1,0},{2,3},{3,2},{4,5},{5,4},{6,7},{7,6},{8,9},{9,8},{10,11... | collective-permute-start | bytes 589832 | tf_op jit(solution)/shard_map/ppermute | solution.py:219
  125.1 16.7 %collective-permute-start.7 = (bf16[256,384]{1,0:T(8,128)(2,1)S(1)}, bf16[256,384]{1,0:T(8,128)(2,1)S(1)}, u32[]{:S(2)}, u32[]{:S(2)}) collective-permute-start(bf16[256,384]{1,0:T(8,128)(2,1)S(1)} %copy-done.21), channel_id=1, source_target_pairs={{0,1},{1,0},{2,3},{3,2},{4,5},{5,4},{6,7},{7,6},{8,9},{9,8},{10,11... | collective-permute-start | bytes 589832 | tf_op jit(solution)/shard_map/ppermute | solution.py:219
  155.1 5.5 %copy-start.3 = (bf16[1024,768]{1,0:T(8,128)(2,1)}, bf16[1024,768]{1,0:T(8,128)(2,1)S(1)}, u32[]{:S(2)}) copy-start(bf16[1024,768]{1,0:T(8,128)(2,1)S(1)} %collective-permute-done.4.refs_1_) | copy-start | bytes 4718596
  157.6 3.0 %copy-start.5 = (bf16[1024,768]{1,0:T(8,128)(2,1)}, bf16[1024,768]{1,0:T(8,128)(2,1)S(1)}, u32[]{:S(2)}) copy-start(bf16[1024,768]{1,0:T(8,128)(2,1)S(1)} %collective-permute-done.5.refs_2_) | copy-start | bytes 4718596
  160.6 0.8 copy-start.13
  161.3 22.0 %collective-permute-start.11 = (bf16[512,768]{1,0:T(8,128)(2,1)}, bf16[512,768]{1,0:T(8,128)(2,1)}, u32[]{:S(2)}, u32[]{:S(2)}) collective-permute-start(bf16[512,768]{1,0:T(8,128)(2,1)} %get-tuple-element.81), channel_id=1, source_target_pairs={{0,6},{1,7},{2,4},{3,5},{4,2},{5,3},{6,0},{7,1},{8,14},{9,15},{10,... | collective-permute-start | bytes 2359304 | tf_op jit(solution)/shard_map/ppermute | solution.py:219
  163.5 20.8 %collective-permute-start.12 = (bf16[512,768]{1,0:T(8,128)(2,1)}, bf16[512,768]{1,0:T(8,128)(2,1)}, u32[]{:S(2)}, u32[]{:S(2)}) collective-permute-start(bf16[512,768]{1,0:T(8,128)(2,1)} %get-tuple-element.82), channel_id=1, source_target_pairs={{0,2},{1,3},{2,0},{3,1},{4,6},{5,7},{6,4},{7,5},{8,10},{9,11},{10,... | collective-permute-start | bytes 2359304 | tf_op jit(solution)/shard_map/ppermute | solution.py:219
  163.5 20.8 %copy-start.2 = (bf16[768,1536]{1,0:T(8,128)(2,1)S(1)}, bf16[768,1536]{1,0:T(8,128)(2,1)}, u32[]{:S(2)}) copy-start(bf16[768,1536]{1,0:T(8,128)(2,1)} %copy-done.1) | copy-start | bytes 7077892
  163.5 20.8 %copy-start.4 = (bf16[1024,768]{1,0:T(8,128)(2,1)S(1)}, bf16[1024,768]{1,0:T(8,128)(2,1)}, u32[]{:S(2)}) copy-start(bf16[1024,768]{1,0:T(8,128)(2,1)} %copy-done.3) | copy-start | bytes 4718596
  168.3 37.3 %collective-permute-start.8 = (bf16[1024,512]{1,0:T(8,128)(2,1)S(1)}, bf16[1024,512]{1,0:T(8,128)(2,1)S(1)}, u32[]{:S(2)}, u32[]{:S(2)}) collective-permute-start(bf16[1024,512]{1,0:T(8,128)(2,1)S(1)} %get-tuple-element.78), channel_id=1, source_target_pairs={{0,2},{1,3},{2,0},{3,1},{4,6},{5,7},{6,4},{7,5},{8,10},{9,11},{10,... | collective-permute-start | bytes 3145736 | tf_op jit(solution)/shard_map/ppermute | solution.py:219
  170.4 35.3 %collective-permute-start.9 = (bf16[1024,512]{1,0:T(8,128)(2,1)S(1)}, bf16[1024,512]{1,0:T(8,128)(2,1)S(1)}, u32[]{:S(2)}, u32[]{:S(2)}) collective-permute-start(bf16[1024,512]{1,0:T(8,128)(2,1)S(1)} %get-tuple-element.79), channel_id=1, source_target_pairs={{0,6},{1,7},{2,4},{3,5},{4,2},{5,3},{6,0},{7,1},{8,14},{9,15},{10,... | collective-permute-start | bytes 3145736 | tf_op jit(solution)/shard_map/ppermute | solution.py:219
  171.4 34.2 %collective-permute-start.10 = (bf16[1024,256]{1,0:T(8,128)(2,1)S(1)}, bf16[1024,256]{1,0:T(8,128)(2,1)S(1)}, u32[]{:S(2)}, u32[]{:S(2)}) collective-permute-start(bf16[1024,256]{1,0:T(8,128)(2,1)S(1)} %get-tuple-element.80), channel_id=1, source_target_pairs={{0,1},{1,0},{2,3},{3,2},{4,5},{5,4},{6,7},{7,6},{8,9},{9,8},{10,11... | collective-permute-start | bytes 1572872 | tf_op jit(solution)/shard_map/ppermute | solution.py:219
  184.3 1.4 copy-start.6
  188.7 12.8 %collective-permute-start.13 = (bf16[256,768]{1,0:T(8,128)(2,1)S(1)}, bf16[256,768]{1,0:T(8,128)(2,1)S(1)}, u32[]{:S(2)}, u32[]{:S(2)}) collective-permute-start(bf16[256,768]{1,0:T(8,128)(2,1)S(1)} %get-tuple-element.86), channel_id=1, source_target_pairs={{0,1},{1,0},{2,3},{3,2},{4,5},{5,4},{6,7},{7,6},{8,9},{9,8},{10,11... | collective-permute-start | bytes 1179656 | tf_op jit(solution)/shard_map/ppermute | solution.py:219
  191.7 13.9 %collective-permute-start.14 = (bf16[256,768]{1,0:T(8,128)(2,1)S(1)}, bf16[256,768]{1,0:T(8,128)(2,1)S(1)}, u32[]{:S(2)}, u32[]{:S(2)}) collective-permute-start(bf16[256,768]{1,0:T(8,128)(2,1)S(1)} %get-tuple-element.87), channel_id=1, source_target_pairs={{0,1},{1,0},{2,3},{3,2},{4,5},{5,4},{6,7},{7,6},{8,9},{9,8},{10,11... | collective-permute-start | bytes 1179656 | tf_op jit(solution)/shard_map/ppermute | solution.py:219
  207.7 11.9 %collective-permute-start.15 = (bf16[512,512]{1,0:T(8,128)(2,1)S(1)}, bf16[512,512]{1,0:T(8,128)(2,1)S(1)}, u32[]{:S(2)}, u32[]{:S(2)}) collective-permute-start(bf16[512,512]{1,0:T(8,128)(2,1)S(1)} %get-tuple-element.89), channel_id=1, source_target_pairs={{0,6},{1,7},{2,4},{3,5},{4,2},{5,3},{6,0},{7,1},{8,14},{9,15},{10,... | collective-permute-start | bytes 1572872 | tf_op jit(solution)/shard_map/ppermute | solution.py:219
  209.6 11.8 %collective-permute-start.16 = (bf16[512,512]{1,0:T(8,128)(2,1)S(1)}, bf16[512,512]{1,0:T(8,128)(2,1)S(1)}, u32[]{:S(2)}, u32[]{:S(2)}) collective-permute-start(bf16[512,512]{1,0:T(8,128)(2,1)S(1)} %get-tuple-element.90), channel_id=1, source_target_pairs={{0,1},{1,0},{2,3},{3,2},{4,5},{5,4},{6,7},{7,6},{8,9},{9,8},{10,11... | collective-permute-start | bytes 1572872 | tf_op jit(solution)/shard_map/ppermute | solution.py:219
  212.3 6.4 %collective-permute-start.17 = (bf16[512,256]{1,0:T(8,128)(2,1)S(1)}, bf16[512,256]{1,0:T(8,128)(2,1)S(1)}, u32[]{:S(2)}, u32[]{:S(2)}) collective-permute-start(bf16[512,256]{1,0:T(8,128)(2,1)S(1)} %get-tuple-element.91), channel_id=1, source_target_pairs={{0,2},{1,3},{2,0},{3,1},{4,6},{5,7},{6,4},{7,5},{8,10},{9,11},{10,... | collective-permute-start | bytes 786440 | tf_op jit(solution)/shard_map/ppermute | solution.py:219
  221.4 11.2 %copy-start.14 = (bf16[256,768]{1,0:T(8,128)(2,1)S(1)}, bf16[256,768]{1,0:T(8,128)(2,1)}, u32[]{:S(2)}) copy-start(bf16[256,768]{1,0:T(8,128)(2,1)} %copy-done.13) | copy-start | bytes 1179652
  223.3 9.0 %collective-permute-start.18 = (bf16[256,512]{1,0:T(8,128)(2,1)S(1)}, bf16[256,512]{1,0:T(8,128)(2,1)S(1)}, u32[]{:S(2)}, u32[]{:S(2)}) collective-permute-start(bf16[256,512]{1,0:T(8,128)(2,1)S(1)} %get-tuple-element.96), channel_id=1, source_target_pairs={{0,1},{1,0},{2,3},{3,2},{4,5},{5,4},{6,7},{7,6},{8,9},{9,8},{10,11... | collective-permute-start | bytes 786440 | tf_op jit(solution)/shard_map/ppermute | solution.py:219
  226.2 6.4 %collective-permute-start.19 = (bf16[256,512]{1,0:T(8,128)(2,1)S(1)}, bf16[256,512]{1,0:T(8,128)(2,1)S(1)}, u32[]{:S(2)}, u32[]{:S(2)}) collective-permute-start(bf16[256,512]{1,0:T(8,128)(2,1)S(1)} %get-tuple-element.97), channel_id=1, source_target_pairs={{0,2},{1,3},{2,0},{3,1},{4,6},{5,7},{6,4},{7,5},{8,10},{9,11},{10,... | collective-permute-start | bytes 786440 | tf_op jit(solution)/shard_map/ppermute | solution.py:219
  226.2 6.2 %collective-permute-start.20 = (bf16[256,256]{1,0:T(8,128)(2,1)S(1)}, bf16[256,256]{1,0:T(8,128)(2,1)S(1)}, u32[]{:S(2)}, u32[]{:S(2)}) collective-permute-start(bf16[256,256]{1,0:T(8,128)(2,1)S(1)} %get-tuple-element.98), channel_id=1, source_target_pairs={{0,6},{1,7},{2,4},{3,5},{4,2},{5,3},{6,0},{7,1},{8,14},{9,15},{10,... | collective-permute-start | bytes 393224 | tf_op jit(solution)/shard_map/ppermute | solution.py:219
